TPU v7x, 32 devices: a whole 2x2x4 slice. The times are simulated.
32 devices in a mesh: grp: 2 (over y), blk: 4 (over z), ch: 2 (over x), sub: 2 (over core).
Axes of the slice: x: 2, y: 2, z: 4, core: 2. Of those that a mesh axis runs over, the one named last changes fastest.
Arguments:
- pair_act: bfloat16 [64, 32, 128], P(('grp', 'blk', 'ch', 'sub')), parts along dimension 0, may hold values from -6 to 6
- pair_grad: bfloat16 [64, 32, 128], P(('grp', 'blk', 'ch', 'sub')), parts along dimension 0, may hold values from -6 to 6
- pair_mask: int32 [64, 32], P(('grp', 'blk', 'ch', 'sub')), parts along dimension 0, may hold values from 0 to 1, as said below
- w_in: bfloat16 [128, 640], replicated, may hold values from -0.5 to 0.5
- w_out: bfloat16 [128, 128], replicated, may hold values from -0.5 to 0.5
- gain_in: float32 [128], replicated, may hold values from 0.5 to 1.5
- bias_in: float32 [128], replicated, may hold values from -2.5 to 2.5
- gain_mid: float32 [128], replicated, may hold values from 0.5 to 1.5
- bias_mid: float32 [128], replicated, may hold values from -2.5 to 2.5
Outputs:
- d_pair: bfloat16 [64, 32, 128], P(('grp', 'blk', 'ch', 'sub')), parts along dimension 0
- d_w_in: float32 [256, 640], P('grp'), parts along dimension 0
- d_w_out: float32 [256, 128], P('grp'), parts along dimension 0
- d_gain_in: float32 [256], P('grp'), parts along dimension 0
- d_bias_in: float32 [256], P('grp'), parts along dimension 0
- d_gain_mid: float32 [256], P('grp'), parts along dimension 0
- d_bias_mid: float32 [256], P('grp'), parts along dimension 0
There are 2 independent parts, one for each index of `grp`. A program takes and returns all parts, laid end to end along the dimension named above; an argument that names none is the same for every part. Nothing has to cross between parts.
Inputs may be any that keep to these rules, and one draw needn't show every extreme that they name: pair_mask[i, j] = v[i] v[j] for one 0/1 vector v over the 32 tokens whose ones all come before its zeros, with at least 16 ones and at least one zero.
All inputs are finite; a program needn't handle non-finite values.
Results may differ from a plain program's by a relative error of at most 0.0089.
Values may be sent and summed in bfloat16 or wider, within the bound.
A program may use at most 64 MiB of HBM per device.

v0:
```python
import jax
import jax.numpy as jnp
from jax import lax
from jax.sharding import PartitionSpec as P


def norm_parts(values):
    center = values - jnp.mean(values, axis=-1, keepdims=True)
    inverse = lax.rsqrt(jnp.mean(center * center, axis=-1, keepdims=True) + 1e-05)
    return (center * inverse, inverse)


def norm_back(upstream, normed, inverse):
    first = jnp.mean(upstream, axis=-1, keepdims=True)
    second = jnp.mean(upstream * normed, axis=-1, keepdims=True)
    return inverse * (upstream - first - normed * second)


def shards(pair_act, pair_grad, pair_mask, w_in, w_out, gain_in, bias_in, gain_mid, bias_mid):
    rows, width, chan = pair_act.shape
    hidden = w_out.shape[0]
    normed, inverse = norm_parts(pair_act.astype(jnp.float32))
    x_low = (normed * gain_in + bias_in).astype(jnp.bfloat16)
    flat_x = x_low.reshape(rows * width, chan)
    proj = jnp.dot(flat_x, w_in, preferred_element_type=jnp.float32).reshape(rows, width, -1)
    maskf = pair_mask.astype(jnp.float32)[:, :, None]
    sig_a = jax.nn.sigmoid(proj[..., :hidden])
    val_a = proj[..., hidden : 2 * hidden]
    sig_b = jax.nn.sigmoid(proj[..., 2 * hidden : 3 * hidden])
    val_b = proj[..., 3 * hidden : 4 * hidden]
    sig_g = jax.nn.sigmoid(proj[..., 4 * hidden :])
    fac_a = (maskf * sig_a * val_a).astype(jnp.bfloat16)
    fac_b = (maskf * sig_b * val_b).astype(jnp.bfloat16)
    stacked = jnp.transpose(jnp.stack([fac_a, fac_b]), (0, 3, 1, 2))
    grouped = lax.all_to_all(stacked, ("ch", "sub"), split_axis=1, concat_axis=2, tiled=True)
    left_loc = grouped[0]
    right_loc = grouped[1]
    stripe = left_loc.shape[1]
    own_start = lax.axis_index("blk") * stripe
    columns = lax.dynamic_slice_in_dim(
        lax.all_gather(left_loc, "blk", axis=1, tiled=True), own_start, stripe, 2
    )
    total = jnp.einsum(
        "hki,hkj->hij",
        columns,
        lax.all_gather(right_loc, "blk", axis=1, tiled=True),
        preferred_element_type=jnp.float32,
    )
    returned_prod = lax.all_to_all(
        total.astype(jnp.bfloat16), ("ch", "sub"), split_axis=1, concat_axis=0, tiled=True
    )
    prod = jnp.transpose(returned_prod, (1, 2, 0)).astype(jnp.float32)
    mid, inverse_mid = norm_parts(prod)
    y_low = (mid * gain_mid + bias_mid).astype(jnp.bfloat16)
    flat_y = y_low.reshape(rows * width, hidden)
    outp = jnp.dot(flat_y, w_out, preferred_element_type=jnp.float32).reshape(rows, width, chan)
    upstream = pair_grad.astype(jnp.float32)
    d_out = (upstream * sig_g).astype(jnp.bfloat16)
    d_sig = upstream * outp
    flat_d = d_out.reshape(rows * width, chan)
    dw_out_part = jnp.dot(flat_y.T, flat_d, preferred_element_type=jnp.float32)
    d_mid = jnp.dot(flat_d, w_out.T, preferred_element_type=jnp.float32).reshape(
        rows, width, hidden
    )
    dgain_mid_part = jnp.sum(d_mid * mid, axis=(0, 1))
    dbias_mid_part = jnp.sum(d_mid, axis=(0, 1))
    mid_totals = lax.psum((dw_out_part, dgain_mid_part, dbias_mid_part), ("blk", "ch", "sub"))
    d_prod = norm_back(d_mid * gain_mid, mid, inverse_mid).astype(jnp.bfloat16)
    d_groups = lax.all_to_all(
        jnp.transpose(d_prod, (2, 0, 1)), ("ch", "sub"), split_axis=0, concat_axis=1, tiled=True
    )
    piece = lax.all_gather(d_groups, "blk", axis=1, tiled=True)
    part_left = jnp.einsum("hkj,hij->hki", right_loc, piece, preferred_element_type=jnp.float32)
    grad_left = part_left
    grad_right = jnp.einsum("hki,hij->hkj", left_loc, piece, preferred_element_type=jnp.float32)
    grad_left, grad_right = (grad_left, grad_right)
    both_grads = jnp.stack([grad_left, grad_right]).astype(jnp.bfloat16)
    returned_grads = lax.all_to_all(
        both_grads, ("ch", "sub"), split_axis=2, concat_axis=1, tiled=True
    )
    pair_grads = jnp.transpose(returned_grads, (0, 2, 3, 1)).astype(jnp.float32)
    grad_a = pair_grads[0]
    grad_b = pair_grads[1]
    d_gate_a = grad_a * maskf * val_a * sig_a * (1.0 - sig_a)
    d_val_a = grad_a * maskf * sig_a
    d_gate_b = grad_b * maskf * val_b * sig_b * (1.0 - sig_b)
    d_val_b = grad_b * maskf * sig_b
    d_gate_g = d_sig * sig_g * (1.0 - sig_g)
    d_proj = jnp.concatenate([d_gate_a, d_val_a, d_gate_b, d_val_b, d_gate_g], axis=-1).astype(
        jnp.bfloat16
    )
    flat_p = d_proj.reshape(rows * width, -1)
    dw_in_part = jnp.dot(flat_x.T, flat_p, preferred_element_type=jnp.float32)
    d_x = jnp.dot(flat_p, w_in.T, preferred_element_type=jnp.float32).reshape(rows, width, chan)
    dgain_in_part = jnp.sum(d_x * normed, axis=(0, 1))
    dbias_in_part = jnp.sum(d_x, axis=(0, 1))
    d_pair = norm_back(d_x * gain_in, normed, inverse).astype(jnp.bfloat16)
    scale = 1.0 / width
    in_totals = lax.psum((dw_in_part, dgain_in_part, dbias_in_part), ("blk", "ch", "sub"))
    sums = (in_totals[0], in_totals[1], in_totals[2], mid_totals[0], mid_totals[1], mid_totals[2])
    return (
        d_pair,
        sums[0] * scale,
        sums[3] * scale,
        sums[1] * scale,
        sums[2] * scale,
        sums[4] * scale,
        sums[5] * scale,
    )


def solution(mesh):
    in_specs = (
        P(("grp", "blk", "ch", "sub"), None, None),
        P(("grp", "blk", "ch", "sub"), None, None),
        P(("grp", "blk", "ch", "sub"), None),
        P(),
        P(),
        P(),
        P(),
        P(),
        P(),
    )
    out_specs = (
        P(("grp", "blk", "ch", "sub"), None, None),
        P("grp", None),
        P("grp", None),
        P("grp"),
        P("grp"),
        P("grp"),
        P("grp"),
    )
    return jax.shard_map(shards, mesh=mesh, in_specs=in_specs, out_specs=out_specs, check_vma=False)
```

profile of v0, /device:TPU:0, one launch (start us, length us, event | category | flops | bytes accessed | tf_op | source)
XLA Modules:
  0.0 215.7 jit_solution(11896415844040118174)
XLA Ops:
  7.2 0.9 convert_reduce_fusion
  8.2 0.7 copy-done.5
  8.9 0.6 copy-done.3
  9.6 0.2 fusion.9
  10.0 0.8 reshape.115
  10.8 4.2 %all-to-all-start = ((bf16[4,2,2048]{2,1,0:T(2,128)(2,1)}), bf16[4,2,2048]{2,1,0:T(2,128)(2,1)S(1)}, u32[]{:S(2)}, u32[]{:S(2)}) async-start(bf16[4,2,2048]{2,1,0:T(2,128)(2,1)} %reshape.115), calls=%async_computation | async-start | bytes 65536 | tf_op jit(solution)/shard_map/all_to_all | solution.py:35
  15.0 3.9 %all-to-all-done = bf16[4,2,2048]{2,1,0:T(2,128)(2,1)S(1)} async-done(((bf16[4,2,2048]{2,1,0:T(2,128)(2,1)}), bf16[4,2,2048]{2,1,0:T(2,128)(2,1)S(1)}, u32[]{:S(2)}, u32[]{:S(2)}) %all-to-all-start) | async-done | bytes 32800 | tf_op jit(solution)/shard_map/all_to_all | solution.py:35
  19.4 14.6 %all_gather.9 = bf16[32,32,32]{2,0,1:T(8,128)(2,1)S(1)} all-gather(bf16[32,8,32]{2,0,1:T(8,128)(2,1)S(1)} %bitcast.113), channel_id=1, replica_groups=mesh['grp'=2,'blk'=4,'ch'=2,'sub'=2] {'blk'}, dimensions={1}, use_global_device_ids=true | all-gather | bytes 81920 | tf_op jit(solution)/shard_map/all_gather | solution.py:41
  34.2 13.3 %all_gather.10 = bf16[32,32,32]{2,1,0:T(8,128)(2,1)S(1)} all-gather(bf16[32,8,32]{2,1,0:T(8,128)(2,1)S(1)} %bitcast.115), channel_id=1, replica_groups=mesh['grp'=2,'blk'=4,'ch'=2,'sub'=2] {'blk'}, dimensions={1}, use_global_device_ids=true | all-gather | bytes 81920 | tf_op jit(solution)/shard_map/all_gather | solution.py:46
  47.6 0.3 convolution_convert_fusion
  48.0 6.2 %all_to_all.51 = bf16[4,2,1024]{2,1,0:T(2,128)(2,1)S(1)} all-to-all(bf16[4,2,1024]{2,1,0:T(2,128)(2,1)S(1)} %reshape.117), channel_id=1, replica_groups=mesh['grp'=2,'blk'=4,'ch'=2,'sub'=2] {'ch','sub'}, dimensions={0} | all-to-all | bytes 32768 | tf_op jit(solution)/shard_map/all_to_all | solution.py:49
  54.8 0.5 copy-done.7
  55.5 0.2 multiply_reduce_fusion
  56.1 6.2 %all_to_all.52 = bf16[4,2,1024]{2,1,0:T(2,128)(2,1)S(1)} all-to-all(bf16[4,2,1024]{2,1,0:T(2,128)(2,1)S(1)} %reshape.119), channel_id=1, replica_groups=mesh['grp'=2,'blk'=4,'ch'=2,'sub'=2] {'ch','sub'}, dimensions={0} | all-to-all | bytes 32768 | tf_op jit(solution)/shard_map/all_to_all | solution.py:69
  62.5 12.8 %all_gather.11 = bf16[32,32,32]{2,1,0:T(8,128)(2,1)S(1)} all-gather(bf16[32,8,32]{2,1,0:T(8,128)(2,1)S(1)} %bitcast.124), channel_id=1, replica_groups=mesh['grp'=2,'blk'=4,'ch'=2,'sub'=2] {'blk'}, dimensions={1}, use_global_device_ids=true | all-gather | bytes 81920 | tf_op jit(solution)/shard_map/all_gather | solution.py:72
  75.3 0.2 fusion
  75.8 0.8 reshape.121
  76.6 3.4 %all-to-all-start.3 = ((bf16[4,2,2048]{2,1,0:T(2,128)(2,1)}), bf16[4,2,2048]{2,1,0:T(2,128)(2,1)S(1)}, u32[]{:S(2)}, u32[]{:S(2)}) async-start(bf16[4,2,2048]{2,1,0:T(2,128)(2,1)} %reshape.121), calls=%async_computation.3 | async-start | bytes 65536 | tf_op jit(solution)/shard_map/all_to_all | solution.py:78
  80.0 0.9 convolution_bitcast_fusion.1
  80.9 3.0 %all-to-all-done.3 = bf16[4,2,2048]{2,1,0:T(2,128)(2,1)S(1)} async-done(((bf16[4,2,2048]{2,1,0:T(2,128)(2,1)}), bf16[4,2,2048]{2,1,0:T(2,128)(2,1)S(1)}, u32[]{:S(2)}, u32[]{:S(2)}) %all-to-all-start.3) | async-done | bytes 32800 | tf_op jit(solution)/shard_map/all_to_all | solution.py:78
  84.7 0.2 fusion.5
  84.9 0.3 fusion.24
  85.2 1.0 convolution_bitcast_fusion
  86.2 30.6 %all-reduce = (f32[128]{0:T(128)S(1)}, f32[128]{0:T(128)S(1)}, f32[128]{0:T(128)S(1)}, f32[128]{0:T(128)S(1)}) all-reduce(f32[128]{0:T(128)S(1)} %get-tuple-element.9, f32[128]{0:T(128)S(1)} %get-tuple-element.14, f32[128]{0:T(128)S(1)} %get-tuple-element.7, ...), channel_id=1, replica_groups=mesh['grp'=2,'blk'=4,'ch'=2,'sub'=2] {'blk','ch','sub'}, use_global_device_ids=true, to_apply=%region_11.0 | all-reduce | flops 512 | bytes 4096 | tf_op jit(solution)/shard_map/psum | solution.py:99
  116.8 0.5 broadcast_multiply_fusion.10
  117.3 0.5 broadcast_multiply_fusion.11
  117.8 0.5 broadcast_multiply_fusion.8
  118.4 0.7 fusion.23
  119.1 0.5 broadcast_multiply_fusion.9
  119.6 86.8 %all-reduce.4.cloned.1.call-done = (f32[128,640]{1,0:T(8,128)}, f32[128,128]{1,0:T(8,128)}) async-done(((f32[128,640]{1,0:T(8,128)}, f32[128,128]{1,0:T(8,128)}), (f32[128,640]{1,0:T(8,128)}, f32[128,128]{1,0:T(8,128)})) %all-reduce.4.cloned.1.call-update) | async-done | bytes 393232 | tf_op jit(solution)/shard_map/psum | solution.py:99
  206.4 1.8 broadcast_multiply_fusion
  208.2 0.6 broadcast_multiply_fusion.1
  (59 shorter events, 3.6 us)
Async XLA Ops:
  7.2 1.8 copy-start
  7.2 0.9 copy-start.1
  8.2 0.7 copy-start.5
  8.9 0.7 copy-start.3
  8.9 0.7 copy-start.4
  10.8 8.2 %all-to-all-start = ((bf16[4,2,2048]{2,1,0:T(2,128)(2,1)}), bf16[4,2,2048]{2,1,0:T(2,128)(2,1)S(1)}, u32[]{:S(2)}, u32[]{:S(2)}) async-start(bf16[4,2,2048]{2,1,0:T(2,128)(2,1)} %reshape.115), calls=%async_computation | async-start | bytes 65536 | tf_op jit(solution)/shard_map/all_to_all | solution.py:35
  54.6 0.8 copy-start.7
  54.7 0.7 copy-start.8
  54.8 0.7 copy-start.6
  76.6 3.5 %copy-start.9 = (f32[128]{0:T(128)S(1)}, f32[128]{0:T(128)}, u32[]{:S(2)}) copy-start(f32[128]{0:T(128)} %param.17) | copy-start | bytes 1540
  76.6 7.3 %all-to-all-start.3 = ((bf16[4,2,2048]{2,1,0:T(2,128)(2,1)}), bf16[4,2,2048]{2,1,0:T(2,128)(2,1)S(1)}, u32[]{:S(2)}, u32[]{:S(2)}) async-start(bf16[4,2,2048]{2,1,0:T(2,128)(2,1)} %reshape.121), calls=%async_computation.3 | async-start | bytes 65536 | tf_op jit(solution)/shard_map/all_to_all | solution.py:78
  80.0 126.5 %all-reduce.4.cloned.1.call-start = ((), (), s32[]{:S(2)}) async-start(), calls=%async_computation.4 | async-start | bytes 786432 | tf_op jit(solution)/shard_map/psum | solution.py:99
  206.4 1.8 copy-start.2
Sparse Core Ops, SparseCore 0:
  118.5 87.8 all-reduce.3
where the time goes:
time: 216 us
  waiting for transfers between devices  93.8 us (43%)
  blocking collectives  83.7 us (39%)
  between operations  14.3 us (7%)
  starting transfers between devices  7.64 us (4%)
  other arithmetic  7.02 us (3%)
  local copies, waits for them, and re-layouts  5.71 us (3%)
  matrix products  3.58 us (2%)
    psum x1, waiting for transfers between devices, shards(): lax.psum((dw_in_part, dgain_in_part, dbias_in_part), ('blk', 'ch', 'sub'))  86.8 us
    psum x1, blocking collectives, shards(): lax.psum((dw_in_part, dgain_in_part, dbias_in_part), ('blk', 'ch', 'sub'))  30.6 us
    all_gather x1, blocking collectives, shards(): lax.all_gather(left_loc, 'blk', axis=1, tiled=True)  14.6 us
    all_gather x1, blocking collectives, shards(): lax.all_gather(right_loc, 'blk', axis=1, tiled=True)  13.3 us
    all_gather x1, blocking collectives, shards(): piece = lax.all_gather(d_groups, 'blk', axis=1, tiled=True)  12.8 us
    all_to_all x1, blocking collectives, shards(): lax.all_to_all(jnp.transpose(d_prod, (2, 0, 1)), ('ch', 'sub'), split_axi...  6.2 us
    all_to_all x1, blocking collectives, shards(): lax.all_to_all(total.astype(jnp.bfloat16), ('ch', 'sub'), split_axis=1, c...  6.2 us
  transfers between devices with their start and end apart: 3, of which 3 were waited for; matrix products, arithmetic and copies ran while one was open for 1% of the time, Pallas kernels for 0%

commit v1 on v0

--- a/solution.py
+++ b/solution.py
@@ -1,6 +1,10 @@
+import functools
+
 import jax
 import jax.numpy as jnp
 from jax import lax
+from jax.experimental import pallas as pl
+from jax.experimental.pallas import tpu as pltpu
 from jax.sharding import PartitionSpec as P
 
 
@@ -109,6 +113,340 @@
     )
 
 
+MESH = pl.DeviceIdType.MESH
+PAD = 16
+VMEM_BYTES = 48 * 1024 * 1024
+
+
+def flat_slot(sizes, blk, ch, sub):
+    return (blk * sizes[1] + ch) * sizes[2] + sub
+
+
+def gather_kernel(sizes, act_ref, grad_ref, mask_ref, ga_ref, gg_ref, send_sem, recv_sem):
+    nz, nx, nc = sizes
+    z, x, c = lax.axis_index("blk"), lax.axis_index("ch"), lax.axis_index("sub")
+    y = lax.axis_index("grp")
+    pairs = act_ref.shape[0]
+    width = mask_ref.shape[1]
+    me = flat_slot(sizes, z, x, c)
+    barrier = pltpu.get_barrier_semaphore()
+    peers_z = [(y, lax.rem(z + s, nz), x, c) for s in range(1, nz)]
+    peers_x = [(y, z, lax.rem(x + s, nx), c) for s in range(1, nx)]
+    peers_c = [(y, z, x, lax.rem(c + s, nc)) for s in range(1, nc)]
+    peers = peers_z + peers_x + peers_c
+    for peer in peers:
+        pl.semaphore_signal(barrier, inc=1, device_id=peer, device_id_type=MESH)
+    ga_ref[me, :pairs, :] = act_ref[...]
+    ga_ref[me, pairs:, :] = jnp.zeros((PAD, act_ref.shape[1]), jnp.bfloat16)
+    ga_ref[me, pairs:, :width] = jnp.broadcast_to(
+        mask_ref[0:1, :].astype(jnp.float32), (PAD, width)
+    ).astype(jnp.bfloat16)
+    gg_ref[me] = grad_ref[...]
+    pl.semaphore_wait(barrier, len(peers))
+
+    bufs = (ga_ref, gg_ref)
+    copies = []
+    counts = [0, 0]
+
+    def push(which, slot, peer):
+        buf = bufs[which]
+        copy = pltpu.make_async_remote_copy(
+            src_ref=buf.at[slot],
+            dst_ref=buf.at[slot],
+            send_sem=send_sem.at[which, counts[which]],
+            recv_sem=recv_sem.at[which, slot],
+            device_id=peer,
+            device_id_type=MESH,
+        )
+        counts[which] += 1
+        copy.start()
+        copies.append(copy)
+
+    def arrived(which, slot):
+        buf = bufs[which]
+        pltpu.make_async_remote_copy(
+            src_ref=buf.at[slot],
+            dst_ref=buf.at[slot],
+            send_sem=send_sem.at[which, 0],
+            recv_sem=recv_sem.at[which, slot],
+            device_id=peers[0],
+            device_id_type=MESH,
+        ).wait_recv()
+
+    for which in (0, 1):
+        for peer in peers_z:
+            push(which, me, peer)
+        for peer in peers_x + peers_c:
+            push(which, me, peer)
+    order_z = [lax.rem(z + s, nz) for s in range(1, nz)]
+    for which in (0, 1):
+        for zz in order_z:
+            slot = flat_slot(sizes, zz, x, c)
+            arrived(which, slot)
+            for peer in peers_x + peers_c:
+                push(which, slot, peer)
+        for s in range(1, nx):
+            xx = lax.rem(x + s, nx)
+            for zz in [z] + order_z:
+                slot = flat_slot(sizes, zz, xx, c)
+                arrived(which, slot)
+                for peer in peers_c:
+                    push(which, slot, peer)
+    for which in (0, 1):
+        for s in range(1, nc):
+            cc = lax.rem(c + s, nc)
+            for xx in [x] + [lax.rem(x + q, nx) for q in range(1, nx)]:
+                for zz in [z] + order_z:
+                    arrived(which, flat_slot(sizes, zz, xx, cc))
+    for copy in copies:
+        copy.wait_send()
+
+
+def lane_mean(values):
+    return jnp.mean(values, axis=-1, keepdims=True)
+
+
+def norm_rows(values):
+    center = values - lane_mean(values)
+    inverse = lax.rsqrt(lane_mean(center * center) + 1e-05)
+    return center * inverse, inverse
+
+
+def sigm(values):
+    return 0.5 * jnp.tanh(0.5 * values) + 0.5
+
+
+def dot_t(left, right):
+    return lax.dot_general(left, right, (((1,), (1,)), ((), ())), preferred_element_type=jnp.float32)
+
+
+def t_dot(left, right):
+    return lax.dot_general(left, right, (((0,), (0,)), ((), ())), preferred_element_type=jnp.float32)
+
+
+def outer_sum(length, row_of, vec_of, width, chan, block):
+    step = 4
+
+    def body(t, acc):
+        acc = list(acc)
+        for s in range(step):
+            q = t * step + s
+            vec = vec_of(q)
+            for p in range(block):
+                acc[p] = acc[p] + row_of(p, q) * vec
+        return tuple(acc)
+
+    zero = jnp.zeros((width, chan), jnp.float32)
+    return lax.fori_loop(0, length // step, body, (zero,) * block)
+
+
+def compute_kernel(
+    sizes, rows, width,
+    ga_ref, gg_ref, w_in_ref, w_out_ref, gain_in_ref, bias_in_ref, gain_mid_ref, bias_mid_ref,
+    d_pair_ref, dw_in_ref, dw_out_ref, dgain_in_ref, dbias_in_ref, dgain_mid_ref, dbias_mid_ref,
+    xs, nrm, fa, fb, ca, cb, qa, qb, sg, ys, dos, dp, dpr, dxs, vc,
+):
+    nz, nx, nc = sizes
+    slots = nz * nx * nc
+    pairs = rows * width
+    chan = w_out_ref.shape[1]
+    hid = w_out_ref.shape[0]
+    scale = 1.0 / width
+    me = flat_slot(sizes, lax.axis_index("blk"), lax.axis_index("ch"), lax.axis_index("sub"))
+
+    lane_v = ga_ref[0, pairs:, :].astype(jnp.float32)[0:1, :]
+    at_row = lax.broadcasted_iota(jnp.int32, (width, chan), 0)
+    at_lane = lax.broadcasted_iota(jnp.int32, (width, chan), 1)
+    diag = jnp.where(at_row == at_lane, jnp.broadcast_to(lane_v, (width, chan)), 0.0)
+    vc[...] = jnp.dot(
+        diag.astype(jnp.bfloat16), jnp.ones((chan, chan), jnp.bfloat16),
+        preferred_element_type=jnp.float32,
+    )
+    gain_in, bias_in = gain_in_ref[...], bias_in_ref[...]
+    gain_mid, bias_mid = gain_mid_ref[...], bias_mid_ref[...]
+
+    per = 2
+
+    def project(t, carry):
+        act = jnp.concatenate([ga_ref[t * per + s, :pairs, :] for s in range(per)], axis=0)
+        size = per * pairs
+        here = pl.ds(pl.multiple_of(t * size, size), size)
+        normed, _ = norm_rows(act.astype(jnp.float32))
+        x_low = (normed * gain_in + bias_in).astype(jnp.bfloat16)
+        nrm[here, :] = normed
+        xs[here, :] = x_low
+        cols = vc[...]
+        mask = jnp.concatenate(
+            [cols * vc[pl.ds(t * per * rows + r, 1), :] for r in range(per * rows)], axis=0
+        )
+        proj = jnp.dot(x_low, w_in_ref[...], preferred_element_type=jnp.float32)
+        for at, fac, coef, gate in ((0, fa, ca, qa), (2, fb, cb, qb)):
+            sig = sigm(proj[:, at * hid : (at + 1) * hid])
+            val = proj[:, (at + 1) * hid : (at + 2) * hid]
+            masked = mask * sig
+            full = masked * val
+            fac[here, :] = full.astype(jnp.bfloat16).astype(jnp.float32)
+            coef[here, :] = masked
+            gate[here, :] = full * (1.0 - sig)
+        sg[here, :] = sigm(proj[:, 4 * hid :])
+        return carry
+
+    lax.fori_loop(0, slots // per, project, 0)
+
+    block = 8
+    big = block * width
+
+    def middle(ib, sums):
+        dgain, dbias = sums
+        base = ib * block
+        total = outer_sum(
+            width,
+            lambda p, k: fa[pl.ds(k * width + base + p, 1), :],
+            lambda k: fb[pl.ds(pl.multiple_of(k * width, width), width), :],
+            width, hid, block,
+        )
+        here = pl.ds(pl.multiple_of(base * width, big), big)
+        prod = jnp.concatenate(total, axis=0).astype(jnp.bfloat16).astype(jnp.float32)
+        mid, inverse = norm_rows(prod)
+        y_low = (mid * gain_mid + bias_mid).astype(jnp.bfloat16)
+        ys[here, :] = y_low
+        per_block = block // rows
+        upstream = jnp.concatenate(
+            [gg_ref[ib * per_block + s] for s in range(per_block)], axis=0
+        ).astype(jnp.float32)
+        sig = sg[here, :]
+        outp = jnp.dot(y_low, w_out_ref[...], preferred_element_type=jnp.float32)
+        d_out = (upstream * sig).astype(jnp.bfloat16)
+        dos[here, :] = d_out
+        dpr[here, 4 * hid :] = (upstream * outp * sig * (1.0 - sig)).astype(jnp.bfloat16)
+        d_mid = dot_t(d_out, w_out_ref[...])
+        dgain = dgain + jnp.sum(d_mid * mid, axis=0, keepdims=True)
+        dbias = dbias + jnp.sum(d_mid, axis=0, keepdims=True)
+        u = d_mid * gain_mid
+        d_prod = inverse * (u - lane_mean(u) - mid * lane_mean(u * mid))
+        dp[here, :] = d_prod.astype(jnp.bfloat16).astype(jnp.float32)
+        return dgain, dbias
+
+    none = jnp.zeros((1, hid), jnp.float32)
+    dgain, dbias = lax.fori_loop(0, width // block, middle, (none, none))
+    dgain_mid_ref[...] = dgain * scale
+    dbias_mid_ref[...] = dbias * scale
+    dw_out_ref[...] = t_dot(ys[...], dos[...]) * scale
+
+    def back(kb, sums):
+        dgain, dbias = sums
+        base = kb * block
+        here = pl.ds(pl.multiple_of(base * width, big), big)
+        left = outer_sum(
+            width,
+            lambda p, j: fb[pl.ds((base + p) * width + j, 1), :],
+            lambda j: dp[pl.ds(j, width, stride=width), :],
+            width, hid, block,
+        )
+        grad = jnp.concatenate(left, axis=0).astype(jnp.bfloat16).astype(jnp.float32)
+        dpr[here, :hid] = (grad * qa[here, :]).astype(jnp.bfloat16)
+        dpr[here, hid : 2 * hid] = (grad * ca[here, :]).astype(jnp.bfloat16)
+        right = outer_sum(
+            width,
+            lambda p, i: fa[pl.ds((base + p) * width + i, 1), :],
+            lambda i: dp[pl.ds(pl.multiple_of(i * width, width), width), :],
+            width, hid, block,
+        )
+        grad = jnp.concatenate(right, axis=0).astype(jnp.bfloat16).astype(jnp.float32)
+        dpr[here, 2 * hid : 3 * hid] = (grad * qb[here, :]).astype(jnp.bfloat16)
+        dpr[here, 3 * hid : 4 * hid] = (grad * cb[here, :]).astype(jnp.bfloat16)
+        d_x = dot_t(dpr[here, :], w_in_ref[...])
+        dxs[here, :] = d_x
+        dgain = dgain + jnp.sum(d_x * nrm[here, :], axis=0, keepdims=True)
+        dbias = dbias + jnp.sum(d_x, axis=0, keepdims=True)
+        return dgain, dbias
+
+    none = jnp.zeros((1, chan), jnp.float32)
+    dgain, dbias = lax.fori_loop(0, width // block, back, (none, none))
+    dgain_in_ref[...] = dgain * scale
+    dbias_in_ref[...] = dbias * scale
+    dw_in_ref[...] = t_dot(xs[...], dpr[...]) * scale
+    _, inverse = norm_rows(ga_ref[me, :pairs, :].astype(jnp.float32))
+    own = pl.ds(pl.multiple_of(me * pairs, pairs), pairs)
+    normed = nrm[own, :]
+    v = dxs[own, :] * gain_in
+    d_pair_ref[...] = (inverse * (v - lane_mean(v) - normed * lane_mean(v * normed))).astype(
+        jnp.bfloat16
+    )
+
+
+def fused(sizes, pair_act, pair_grad, pair_mask, w_in, w_out, gain_in, bias_in, gain_mid, bias_mid):
+    rows, width, chan = pair_act.shape
+    hid = w_out.shape[0]
+    pairs = rows * width
+    slots = sizes[0] * sizes[1] * sizes[2]
+    sends = sizes[0] - 1 + sizes[0] * (sizes[1] - 1) + sizes[0] * sizes[1] * (sizes[2] - 1)
+    vmem = pl.BlockSpec(memory_space=pltpu.VMEM)
+    ga, gg = pl.pallas_call(
+        functools.partial(gather_kernel, sizes),
+        out_shape=(
+            jax.ShapeDtypeStruct((slots, pairs + PAD, chan), jnp.bfloat16),
+            jax.ShapeDtypeStruct((slots, pairs, chan), jnp.bfloat16),
+        ),
+        in_specs=[vmem] * 3,
+        out_specs=(vmem, vmem),
+        scratch_shapes=[
+            pltpu.SemaphoreType.DMA((2, sends)),
+            pltpu.SemaphoreType.DMA((2, slots)),
+        ],
+        compiler_params=pltpu.CompilerParams(
+            collective_id=0, has_side_effects=True, vmem_limit_bytes=VMEM_BYTES
+        ),
+    )(pair_act.reshape(pairs, chan), pair_grad.reshape(pairs, chan), pair_mask)
+    full = slots * pairs
+    f32, low = jnp.float32, jnp.bfloat16
+    out = pl.pallas_call(
+        functools.partial(compute_kernel, sizes, rows, width),
+        out_shape=(
+            jax.ShapeDtypeStruct((pairs, chan), low),
+            jax.ShapeDtypeStruct(w_in.shape, f32),
+            jax.ShapeDtypeStruct(w_out.shape, f32),
+            jax.ShapeDtypeStruct((1, chan), f32),
+            jax.ShapeDtypeStruct((1, chan), f32),
+            jax.ShapeDtypeStruct((1, hid), f32),
+            jax.ShapeDtypeStruct((1, hid), f32),
+        ),
+        in_specs=[vmem] * 8,
+        out_specs=(vmem,) * 7,
+        scratch_shapes=[
+            pltpu.VMEM((full, chan), low),
+            pltpu.VMEM((full, chan), f32),
+        ]
+        + [pltpu.VMEM((full, hid), f32)] * 6
+        + [
+            pltpu.VMEM((full, chan), f32),
+            pltpu.VMEM((full, hid), low),
+            pltpu.VMEM((full, chan), low),
+            pltpu.VMEM((full, hid), f32),
+            pltpu.VMEM((full, w_in.shape[1]), low),
+            pltpu.VMEM((full, chan), f32),
+            pltpu.VMEM((width, hid), f32),
+        ],
+        compiler_params=pltpu.CompilerParams(vmem_limit_bytes=VMEM_BYTES),
+    )(
+        ga, gg, w_in, w_out, gain_in.reshape(1, chan), bias_in.reshape(1, chan),
+        gain_mid.reshape(1, hid), bias_mid.reshape(1, hid),
+    )
+    return (out[0].reshape(rows, width, chan), out[1], out[2]) + tuple(
+        piece.reshape(-1) for piece in out[3:]
+    )
+
+
+def choose(mesh, *args):
+    rows, width, chan = args[0].shape
+    sizes = (mesh.shape["blk"], mesh.shape["ch"], mesh.shape["sub"])
+    fits = width * width * chan * 64 <= VMEM_BYTES // 2
+    whole = width % 32 == 0 and 8 % rows == 0 and chan == 128 and args[4].shape[0] == 128
+    if fits and whole and rows * sizes[0] * sizes[1] * sizes[2] == width:
+        return fused(sizes, *args)
+    return shards(*args)
+
+
 def solution(mesh):
     in_specs = (
         P(("grp", "blk", "ch", "sub"), None, None),
@@ -130,4 +468,5 @@
         P("grp"),
         P("grp"),
     )
-    return jax.shard_map(shards, mesh=mesh, in_specs=in_specs, out_specs=out_specs, check_vma=False)
+    body = functools.partial(choose, mesh)
+    return jax.shard_map(body, mesh=mesh, in_specs=in_specs, out_specs=out_specs, check_vma=False)

time: 216 us -> 33.4 us (0.15)
  waiting for transfers between devices: 93.8 us -> 0 us
  blocking collectives: 83.7 us -> 0 us
  Pallas kernels: 0 us -> 28.6 us
  between operations: 14.3 us -> 0.7 us
  starting transfers between devices: 7.64 us -> 0 us
  other arithmetic: 7.02 us -> 0 us
  matrix products: 3.58 us -> 0 us
    psum x1 -> x0, waiting for transfers between devices: 86.8 us -> none  [shards(): lax.psum((dw_in_part, dgain_in_part, dbias_in_part), ('blk', 'ch', 'sub'))]
    all_gather x3 -> x0, blocking collectives: 40.7 us -> none  [the longest x1 14.6 us: shards(): lax.all_gather(left_loc, 'blk', axis=1, tiled=True)]
    psum x1 -> x0, blocking collectives: 30.6 us -> none  [shards(): lax.psum((dw_in_part, dgain_in_part, dbias_in_part), ('blk', 'ch', 'sub'))]
    pallas_call x0 -> x2, Pallas kernels: none -> 28.6 us  [the longest x1 15.8 us: fused(): pl.pallas_call(functools.partial(gather_kernel, sizes), out_shape=(jax.Sh...]
    all_to_all x2 -> x0, blocking collectives: 12.4 us -> none  [the longest x1 6.2 us: shards(): lax.all_to_all(jnp.transpose(d_prod, (2, 0, 1)), ('ch', 'sub'), split_axi...]
    all_to_all x2 -> x0, starting transfers between devices: 7.6 us -> none  [the longest x1 4.21 us: shards(): lax.all_to_all(stacked, ('ch', 'sub'), split_axis=1, concat_axis=2, tiled...]
    all_to_all x2 -> x0, waiting for transfers between devices: 6.9 us -> none  [the longest x1 3.95 us: shards(): lax.all_to_all(stacked, ('ch', 'sub'), split_axis=1, concat_axis=2, tiled...]
    mul x6 -> x0, other arithmetic: 4.44 us -> none  [the longest x1 1.75 us: shards(): sums[0] * scale]
  transfers between devices with their start and end apart: 3 -> 0, of which waited for: 3 -> 0; matrix products, arithmetic and copies ran while one was open for 1% -> 0% of each run, Pallas kernels for 0% -> 0%
where the time goes in v1:
time: 33.4 us; the launch traced here: 33 us
  Pallas kernels  28.6 us (86%)
  local copies, waits for them, and re-layouts  3.69 us (11%)
  between operations  0.7 us (2%)
    pallas_call x1, Pallas kernels, fused(): pl.pallas_call(functools.partial(gather_kernel, sizes), out_shape=(jax.Sh...  15.8 us
    pallas_call x1, Pallas kernels, fused(): pl.pallas_call(functools.partial(compute_kernel, sizes, rows, width), out...  12.9 us
    unnamed x18, local copies, waits for them, and re-layouts  3.69 us

profile of v1, /device:TPU:0, one launch (start us, length us, event | category | flops | bytes accessed | tf_op | source)
XLA Modules:
  0.0 33.0 jit_solution(9025220523204150173)
XLA Ops:
  0.6 0.0 copy-start.1
  0.6 0.0 copy-start.2
  0.7 0.7 %copy-done.2 = bf16[2,32,128]{2,1,0:T(8,128)(2,1)S(1)} copy-done((bf16[2,32,128]{2,1,0:T(8,128)(2,1)S(1)}, bf16[2,32,128]{2,1,0:T(8,128)(2,1)}, u32[]{:S(2)}) %copy-start.2) | copy-done | bytes 16408
  1.4 0.0 copy-start.3
  1.4 0.7 %copy-done.3 = bf16[2,32,128]{2,1,0:T(8,128)(2,1)S(1)} copy-done((bf16[2,32,128]{2,1,0:T(8,128)(2,1)S(1)}, bf16[2,32,128]{2,1,0:T(8,128)(2,1)}, u32[]{:S(2)}) %copy-start.3) | copy-done | bytes 16408
  2.1 0.0 copy-start.4
  2.1 0.7 %copy-done.4 = s32[2,32]{1,0:T(2,128)S(1)} copy-done((s32[2,32]{1,0:T(2,128)S(1)}, s32[2,32]{1,0:T(2,128)}, u32[]{:S(2)}) %copy-start.4) | copy-done | bytes 280
  2.8 15.8 %shard_map.144 = (bf16[16,80,128]{2,1,0:T(8,128)(2,1)S(1)}, bf16[16,64,128]{2,1,0:T(8,128)(2,1)S(1)}) custom-call(bf16[64,128]{1,0:T(8,128)(2,1)S(1)} %bitcast.11, bf16[64,128]{1,0:T(8,128)(2,1)S(1)} %bitcast.12, s32[2,32]{1,0:T(2,128)S(1)} %copy-done.4), custom_call_target="tpu_custom_call" | custom-call | tf_op jit(solution)/shard_map/pallas_call | solution.py:385
  18.5 0.0 copy-start.8
  18.6 0.0 copy-start.5
  18.6 0.0 copy-start.6
  18.6 0.0 copy-start.7
  18.6 0.0 copy-done.1
  18.6 0.6 %copy-done.8 = f32[128]{0:T(128)S(1)} copy-done((f32[128]{0:T(128)S(1)}, f32[128]{0:T(128)}, u32[]{:S(2)}) %copy-start.8) | copy-done | bytes 536
  19.2 0.0 copy-done.5
  19.2 0.0 copy-done.6
  19.2 0.0 copy-done.7
  19.2 0.0 copy-start
  19.3 0.9 %copy-done = bf16[128,640]{1,0:T(8,128)(2,1)S(1)} copy-done((bf16[128,640]{1,0:T(8,128)(2,1)S(1)}, bf16[128,640]{1,0:T(8,128)(2,1)}, u32[]{:S(2)}) %copy-start) | copy-done | bytes 163864
  20.2 12.9 %shard_map.145 = (bf16[64,128]{1,0:T(8,128)(2,1)}, f32[128,640]{1,0:T(8,128)}, f32[128,128]{1,0:T(8,128)}, f32[1,128]{1,0:T(1,128)}, f32[1,128]{1,0:T(1,128)}, /*index=5*/f32[1,128]{1,0:T(1,128)}, f32[1,128]{1,0:T(1,128)}) custom-call(bf16[16,80,128]{2,1,0:T(8,128)(2,1)S(1)} %get-tuple-element.16.ga_ref, bf16[16,64,128]{2,1,0:T(8,128)(2,1)S(1)} %get-tuple-element.17.gg_ref, ...), custom_call_target="tpu_custom_call" | custom-call | tf_op jit(solution)/shard_map/pallas_call | solution.py:403
Async XLA Ops:
  0.6 18.0 %copy-start.1 = (bf16[128,128]{1,0:T(8,128)(2,1)S(1)}, bf16[128,128]{1,0:T(8,128)(2,1)}, u32[]{:S(2)}) copy-start(bf16[128,128]{1,0:T(8,128)(2,1)} %w_out_ref.1) | copy-start | bytes 98308
  0.6 0.7 %copy-start.2 = (bf16[2,32,128]{2,1,0:T(8,128)(2,1)S(1)}, bf16[2,32,128]{2,1,0:T(8,128)(2,1)}, u32[]{:S(2)}) copy-start(bf16[2,32,128]{2,1,0:T(8,128)(2,1)} %param.9) | copy-start | bytes 49156
  1.4 0.7 %copy-start.3 = (bf16[2,32,128]{2,1,0:T(8,128)(2,1)S(1)}, bf16[2,32,128]{2,1,0:T(8,128)(2,1)}, u32[]{:S(2)}) copy-start(bf16[2,32,128]{2,1,0:T(8,128)(2,1)} %param.10) | copy-start | bytes 49156
  2.1 0.7 %copy-start.4 = (s32[2,32]{1,0:T(2,128)S(1)}, s32[2,32]{1,0:T(2,128)}, u32[]{:S(2)}) copy-start(s32[2,32]{1,0:T(2,128)} %mask_ref.1) | copy-start | bytes 772
  18.5 0.7 %copy-start.8 = (f32[128]{0:T(128)S(1)}, f32[128]{0:T(128)}, u32[]{:S(2)}) copy-start(f32[128]{0:T(128)} %param.17) | copy-start | bytes 1540
  18.6 0.7 %copy-start.5 = (f32[128]{0:T(128)S(1)}, f32[128]{0:T(128)}, u32[]{:S(2)}) copy-start(f32[128]{0:T(128)} %param.14) | copy-start | bytes 1540
  18.6 0.7 %copy-start.6 = (f32[128]{0:T(128)S(1)}, f32[128]{0:T(128)}, u32[]{:S(2)}) copy-start(f32[128]{0:T(128)} %param.15) | copy-start | bytes 1540
  18.6 0.7 %copy-start.7 = (f32[128]{0:T(128)S(1)}, f32[128]{0:T(128)}, u32[]{:S(2)}) copy-start(f32[128]{0:T(128)} %param.16) | copy-start | bytes 1540
  19.2 0.9 %copy-start = (bf16[128,640]{1,0:T(8,128)(2,1)S(1)}, bf16[128,640]{1,0:T(8,128)(2,1)}, u32[]{:S(2)}) copy-start(bf16[128,640]{1,0:T(8,128)(2,1)} %w_in_ref.1) | copy-start | bytes 491524

commit v2 on v0

--- a/solution.py
+++ b/solution.py
@@ -1,6 +1,10 @@
+import functools
+
 import jax
 import jax.numpy as jnp
 from jax import lax
+from jax.experimental import pallas as pl
+from jax.experimental.pallas import tpu as pltpu
 from jax.sharding import PartitionSpec as P
 
 
@@ -109,6 +113,388 @@
     )
 
 
+MESH = pl.DeviceIdType.MESH
+PAD = 16
+VMEM_BYTES = 32 * 1024 * 1024
+
+
+def flat_slot(sizes, blk, ch, sub):
+    return (blk * sizes[1] + ch) * sizes[2] + sub
+
+
+def lane_mean(values):
+    return jnp.mean(values, axis=-1, keepdims=True)
+
+
+def norm_rows(values):
+    center = values - lane_mean(values)
+    inverse = lax.rsqrt(lane_mean(center * center) + 1e-05)
+    return center * inverse, inverse
+
+
+def sigm(values):
+    return 0.5 * jnp.tanh(0.5 * values) + 0.5
+
+
+def dot_t(left, right):
+    return lax.dot_general(left, right, (((1,), (1,)), ((), ())), preferred_element_type=jnp.float32)
+
+
+def t_dot(left, right):
+    return lax.dot_general(left, right, (((0,), (0,)), ((), ())), preferred_element_type=jnp.float32)
+
+
+def outer_sum(length, row_of, vec_of, width, chan, block):
+    step = 4
+
+    def body(t, acc):
+        acc = list(acc)
+        for s in range(step):
+            q = t * step + s
+            vec = vec_of(q)
+            for p in range(block):
+                acc[p] = acc[p] + row_of(p, q) * vec
+        return tuple(acc)
+
+    zero = jnp.zeros((width, chan), jnp.float32)
+    return lax.fori_loop(0, length // step, body, (zero,) * block)
+
+
+def front_kernel(
+    sizes, rows, width,
+    act_hbm, grad_hbm, mask_hbm, w_in_hbm, w_out_hbm, gain_in_ref, bias_in_ref, gain_mid_ref, bias_mid_ref,
+    xs, nrm, fa, fb, ca, cb, qa, qb, dp, dpg, dw_out_ref, dgain_mid_ref, dbias_mid_ref,
+    ga, gg, mask_ref, w_in_ref, w_out_ref, sg, ys, dos, in_sem, send_sem, recv_sem, core_send,
+):
+    nz, nx, nc = sizes
+    chips = nz * nx
+    pairs = rows * width
+    chan = w_out_ref.shape[1]
+    hid = w_out_ref.shape[0]
+    scale = 1.0 / width
+    z, x, c = lax.axis_index("blk"), lax.axis_index("ch"), lax.axis_index("sub")
+    y = lax.axis_index("grp")
+    me = flat_slot(sizes, z, x, c)
+    barrier = pltpu.get_barrier_semaphore()
+    others = [
+        (lax.rem(z + s, nz), lax.rem(x + r, nx))
+        for r in range(nx) for s in range(nz) if s or r
+    ]
+    peers = [(y, zz, xx, c) for zz, xx in others]
+    cores = [(y, z, x, lax.rem(c + s, nc)) for s in range(1, nc)]
+    for peer in peers + cores:
+        pl.semaphore_signal(barrier, inc=1, device_id=peer, device_id_type=MESH)
+    loads = [
+        pltpu.make_async_copy(act_hbm, ga.at[me, pl.ds(0, pairs)], in_sem.at[0]),
+        pltpu.make_async_copy(mask_hbm, mask_ref, in_sem.at[1]),
+        pltpu.make_async_copy(grad_hbm, gg.at[me], in_sem.at[2]),
+        pltpu.make_async_copy(w_in_hbm, w_in_ref, in_sem.at[3]),
+        pltpu.make_async_copy(w_out_hbm, w_out_ref, in_sem.at[4]),
+    ]
+    for load in loads:
+        load.start()
+    loads[1].wait()
+    ga[me, pairs:, :] = jnp.zeros((PAD, chan), jnp.bfloat16)
+    mine = mask_ref[...].astype(jnp.float32)
+    ga[me, pairs:, :width] = jnp.concatenate(
+        [jnp.broadcast_to(mine[r : r + 1, :], (PAD // rows, width)) for r in range(rows)], axis=0
+    ).astype(jnp.bfloat16)
+    loads[0].wait()
+    pl.semaphore_wait(barrier, len(peers) + len(cores))
+
+    bufs = (ga, gg)
+
+    def chip_copy(which, slot, n, peer):
+        return pltpu.make_async_remote_copy(
+            src_ref=bufs[which].at[slot], dst_ref=bufs[which].at[slot],
+            send_sem=send_sem.at[which, n], recv_sem=recv_sem.at[which, slot],
+            device_id=peer, device_id_type=MESH,
+        )
+
+    def core_copy(which, slot, n):
+        return pltpu.make_async_remote_copy(
+            src_ref=bufs[which].at[slot], dst_ref=bufs[which].at[slot],
+            send_sem=core_send.at[which, n], recv_sem=recv_sem.at[which, slot],
+            device_id=cores[n // chips], device_id_type=MESH,
+        )
+
+    def send_own(which):
+        for n, peer in enumerate(peers):
+            chip_copy(which, me, n, peer).start()
+        for k in range(nc - 1):
+            core_copy(which, me, k * chips).start()
+
+    def take(which, n):
+        zz, xx = others[n - 1]
+        slot = flat_slot(sizes, zz, xx, c)
+        chip_copy(which, slot, 0, peers[0]).wait_recv()
+        for k in range(nc - 1):
+            core_copy(which, slot, k * chips + n).start()
+
+    def take_core(which, slot):
+        chip_copy(which, slot, 0, peers[0]).wait_recv()
+
+    send_own(0)
+    gain_in, bias_in = gain_in_ref[...], bias_in_ref[...]
+    gain_mid, bias_mid = gain_mid_ref[...], bias_mid_ref[...]
+    at_row = lax.broadcasted_iota(jnp.int32, (width, chan), 0)
+    at_lane = lax.broadcasted_iota(jnp.int32, (width, chan), 1)
+    on_diag = at_row == at_lane
+    ones = jnp.ones((chan, chan), jnp.bfloat16)
+
+    def project(slots):
+        act = jnp.concatenate([ga[s, :pairs, :] for s in slots], axis=0)
+        lines = [ga[s, pairs:, :].astype(jnp.float32) for s in slots]
+        diag = [
+            jnp.where(on_diag, jnp.broadcast_to(line[r * (PAD // rows)][None, :], (width, chan)), 0.0)
+            for line in lines for r in range(rows)
+        ]
+        mask = jnp.dot(
+            jnp.concatenate(diag, axis=0).astype(jnp.bfloat16), ones,
+            preferred_element_type=jnp.float32,
+        )
+        normed, _ = norm_rows(act.astype(jnp.float32))
+        x_low = (normed * gain_in + bias_in).astype(jnp.bfloat16)
+
+        def put(ref, value):
+            for p, s in enumerate(slots):
+                ref[pl.ds(pl.multiple_of(s * pairs, pairs), pairs), :] = value[
+                    p * pairs : (p + 1) * pairs
+                ]
+
+        put(nrm, normed)
+        put(xs, x_low)
+        proj = jnp.dot(x_low, w_in_ref[...], preferred_element_type=jnp.float32)
+        for at, fac, coef, gate in ((0, fa, ca, qa), (2, fb, cb, qb)):
+            sig = sigm(proj[:, at * hid : (at + 1) * hid])
+            val = proj[:, (at + 1) * hid : (at + 2) * hid]
+            masked = mask * sig
+            full = masked * val
+            put(fac, full.astype(jnp.bfloat16).astype(jnp.float32))
+            put(coef, masked)
+            put(gate, full * (1.0 - sig))
+        put(sg, sigm(proj[:, 4 * hid :]))
+
+    loads[3].wait()
+    loads[2].wait()
+    for n in range(1, nz):
+        take(0, n)
+    send_own(1)
+    for r in range(nx):
+        if r:
+            for n in range(r * nz, (r + 1) * nz):
+                take(0, n)
+        xx = lax.rem(x + r, nx)
+        project([flat_slot(sizes, lax.rem(z + s, nz), xx, c) for s in range(nz)])
+    for k in range(1, nc):
+        cc = lax.rem(c + k, nc)
+        for r in range(nx):
+            xx = lax.rem(x + r, nx)
+            slots = [flat_slot(sizes, lax.rem(z + s, nz), xx, cc) for s in range(nz)]
+            for slot in slots:
+                take_core(0, slot)
+            project(slots)
+    for n in range(1, chips):
+        take(1, n)
+    loads[4].wait()
+
+    block = 8
+    big = block * width
+
+    def product(ib, carry):
+        base = ib * block
+        total = outer_sum(
+            width,
+            lambda p, k: fa[pl.ds(k * width + base + p, 1), :],
+            lambda k: fb[pl.ds(pl.multiple_of(k * width, width), width), :],
+            width, hid, block,
+        )
+        dp[pl.ds(pl.multiple_of(base * width, big), big), :] = jnp.concatenate(total, axis=0)
+        return carry
+
+    lax.fori_loop(0, width // block, product, 0)
+    for k in range(1, nc):
+        cc = lax.rem(c + k, nc)
+        for zz, xx in [(z, x)] + others:
+            take_core(1, flat_slot(sizes, zz, xx, cc))
+
+    def middle(ib, sums):
+        dgain, dbias = sums
+        here = pl.ds(pl.multiple_of(ib * big, big), big)
+        prod = dp[here, :].astype(jnp.bfloat16).astype(jnp.float32)
+        mid, inverse = norm_rows(prod)
+        y_low = (mid * gain_mid + bias_mid).astype(jnp.bfloat16)
+        ys[here, :] = y_low
+        per_block = block // rows
+        upstream = jnp.concatenate(
+            [gg[ib * per_block + s] for s in range(per_block)], axis=0
+        ).astype(jnp.float32)
+        sig = sg[here, :]
+        outp = jnp.dot(y_low, w_out_ref[...], preferred_element_type=jnp.float32)
+        d_out = (upstream * sig).astype(jnp.bfloat16)
+        dos[here, :] = d_out
+        dpg[here, :] = (upstream * outp * sig * (1.0 - sig)).astype(jnp.bfloat16)
+        d_mid = dot_t(d_out, w_out_ref[...])
+        dgain = dgain + jnp.sum(d_mid * mid, axis=0, keepdims=True)
+        dbias = dbias + jnp.sum(d_mid, axis=0, keepdims=True)
+        u = d_mid * gain_mid
+        d_prod = inverse * (u - lane_mean(u) - mid * lane_mean(u * mid))
+        dp[here, :] = d_prod.astype(jnp.bfloat16).astype(jnp.float32)
+        return dgain, dbias
+
+    none = jnp.zeros((1, hid), jnp.float32)
+    dgain, dbias = lax.fori_loop(0, width // block, middle, (none, none))
+    dgain_mid_ref[...] = dgain * scale
+    dbias_mid_ref[...] = dbias * scale
+    dw_out_ref[...] = t_dot(ys[...], dos[...]) * scale
+    for which in (0, 1):
+        for n, peer in enumerate(peers):
+            chip_copy(which, me, n, peer).wait_send()
+        for n in range((nc - 1) * chips):
+            core_copy(which, me, n).wait_send()
+
+
+def back_kernel(
+    sizes, rows, width,
+    xs, nrm, fa, fb, ca, cb, qa, qb, dp, dpg, dwo, dgm, dbm, act_hbm, w_in_hbm, gain_in_ref,
+    d_pair_ref, dw_in_ref, dw_out_ref, dgain_in_ref, dbias_in_ref, dgain_mid_ref, dbias_mid_ref,
+    dpr, dxs, act_ref, w_in_ref, in_sem,
+):
+    pairs = rows * width
+    hid, chan = fa.shape[1], nrm.shape[1]
+    scale = 1.0 / width
+    loads = [
+        pltpu.make_async_copy(w_in_hbm, w_in_ref, in_sem.at[0]),
+        pltpu.make_async_copy(act_hbm, act_ref, in_sem.at[1]),
+    ]
+    for load in loads:
+        load.start()
+    me = flat_slot(sizes, lax.axis_index("blk"), lax.axis_index("ch"), lax.axis_index("sub"))
+    dw_out_ref[...] = dwo[...]
+    dgain_mid_ref[...] = dgm[...]
+    dbias_mid_ref[...] = dbm[...]
+    for load in loads:
+        load.wait()
+    block = 8
+    big = block * width
+
+    def back(kb, sums):
+        dgain, dbias = sums
+        base = kb * block
+        here = pl.ds(pl.multiple_of(base * width, big), big)
+        left = outer_sum(
+            width,
+            lambda p, j: fb[pl.ds((base + p) * width + j, 1), :],
+            lambda j: dp[pl.ds(j, width, stride=width), :],
+            width, hid, block,
+        )
+        grad = jnp.concatenate(left, axis=0).astype(jnp.bfloat16).astype(jnp.float32)
+        dpr[here, :hid] = (grad * qa[here, :]).astype(jnp.bfloat16)
+        dpr[here, hid : 2 * hid] = (grad * ca[here, :]).astype(jnp.bfloat16)
+        right = outer_sum(
+            width,
+            lambda p, i: fa[pl.ds((base + p) * width + i, 1), :],
+            lambda i: dp[pl.ds(pl.multiple_of(i * width, width), width), :],
+            width, hid, block,
+        )
+        grad = jnp.concatenate(right, axis=0).astype(jnp.bfloat16).astype(jnp.float32)
+        dpr[here, 2 * hid : 3 * hid] = (grad * qb[here, :]).astype(jnp.bfloat16)
+        dpr[here, 3 * hid : 4 * hid] = (grad * cb[here, :]).astype(jnp.bfloat16)
+        dpr[here, 4 * hid :] = dpg[here, :]
+        d_x = dot_t(dpr[here, :], w_in_ref[...])
+        dxs[here, :] = d_x
+        dgain = dgain + jnp.sum(d_x * nrm[here, :], axis=0, keepdims=True)
+        dbias = dbias + jnp.sum(d_x, axis=0, keepdims=True)
+        return dgain, dbias
+
+    none = jnp.zeros((1, chan), jnp.float32)
+    dgain, dbias = lax.fori_loop(0, width // block, back, (none, none))
+    dgain_in_ref[...] = dgain * scale
+    dbias_in_ref[...] = dbias * scale
+    dw_in_ref[...] = t_dot(xs[...], dpr[...]) * scale
+    _, inverse = norm_rows(act_ref[...].astype(jnp.float32))
+    own = pl.ds(pl.multiple_of(me * pairs, pairs), pairs)
+    normed = nrm[own, :]
+    v = dxs[own, :] * gain_in_ref[...]
+    d_pair_ref[...] = (inverse * (v - lane_mean(v) - normed * lane_mean(v * normed))).astype(
+        jnp.bfloat16
+    )
+
+
+def fused(sizes, pair_act, pair_grad, pair_mask, w_in, w_out, gain_in, bias_in, gain_mid, bias_mid):
+    rows, width, chan = pair_act.shape
+    hid = w_out.shape[0]
+    pairs = rows * width
+    chips = sizes[0] * sizes[1]
+    slots = chips * sizes[2]
+    full = slots * pairs
+    f32, low = jnp.float32, jnp.bfloat16
+    vmem = pl.BlockSpec(memory_space=pltpu.VMEM)
+    hbm = pl.BlockSpec(memory_space=pltpu.HBM)
+    act = pair_act.reshape(pairs, chan)
+    gain_row = gain_in.reshape(1, chan)
+    vector = jax.ShapeDtypeStruct((1, hid), f32)
+    big = jax.ShapeDtypeStruct((full, hid), f32)
+    big_low = jax.ShapeDtypeStruct((full, hid), low)
+    kept = pl.pallas_call(
+        functools.partial(front_kernel, sizes, rows, width),
+        out_shape=(big_low,) + (big,) * 8 + (big_low, jax.ShapeDtypeStruct(w_out.shape, f32), vector, vector),
+        in_specs=[hbm] * 5 + [vmem] * 4,
+        out_specs=(vmem,) * 13,
+        scratch_shapes=[
+            pltpu.VMEM((slots, pairs + PAD, chan), low),
+            pltpu.VMEM((slots, pairs, chan), low),
+            pltpu.VMEM((rows, width), jnp.int32),
+            pltpu.VMEM(w_in.shape, low),
+            pltpu.VMEM(w_out.shape, low),
+            pltpu.VMEM((full, chan), f32),
+            pltpu.VMEM((full, hid), low),
+            pltpu.VMEM((full, chan), low),
+            pltpu.SemaphoreType.DMA((5,)),
+            pltpu.SemaphoreType.DMA((2, chips)),
+            pltpu.SemaphoreType.DMA((2, slots)),
+            pltpu.SemaphoreType.DMA((2, slots)),
+        ],
+        compiler_params=pltpu.CompilerParams(
+            collective_id=0, has_side_effects=True, vmem_limit_bytes=VMEM_BYTES
+        ),
+    )(
+        act, pair_grad.reshape(pairs, chan), pair_mask, w_in, w_out, gain_row,
+        bias_in.reshape(1, chan), gain_mid.reshape(1, hid), bias_mid.reshape(1, hid),
+    )
+    out = pl.pallas_call(
+        functools.partial(back_kernel, sizes, rows, width),
+        out_shape=(
+            jax.ShapeDtypeStruct((pairs, chan), low),
+            jax.ShapeDtypeStruct(w_in.shape, f32),
+            jax.ShapeDtypeStruct(w_out.shape, f32),
+        ) + (vector,) * 4,
+        in_specs=[vmem] * 13 + [hbm, hbm, vmem],
+        out_specs=(vmem,) * 7,
+        scratch_shapes=[
+            pltpu.VMEM((full, w_in.shape[1]), low),
+            pltpu.VMEM((full, chan), f32),
+            pltpu.VMEM((pairs, chan), low),
+            pltpu.VMEM(w_in.shape, low),
+            pltpu.SemaphoreType.DMA((2,)),
+        ],
+        compiler_params=pltpu.CompilerParams(vmem_limit_bytes=VMEM_BYTES),
+    )(*kept, act, w_in, gain_row)
+    return (out[0].reshape(rows, width, chan), out[1], out[2]) + tuple(
+        piece.reshape(-1) for piece in out[3:]
+    )
+
+
+def choose(mesh, *args):
+    rows, width, chan = args[0].shape
+    sizes = (mesh.shape["blk"], mesh.shape["ch"], mesh.shape["sub"])
+    fits = width * width * chan * 128 <= VMEM_BYTES
+    whole = width % 32 == 0 and 8 % rows == 0 and chan >= width and chan == 128 and args[4].shape[0] == 128
+    if fits and whole and rows * sizes[0] * sizes[1] * sizes[2] == width:
+        return fused(sizes, *args)
+    return shards(*args)
+
+
 def solution(mesh):
     in_specs = (
         P(("grp", "blk", "ch", "sub"), None, None),
@@ -130,4 +516,5 @@
         P("grp"),
         P("grp"),
     )
-    return jax.shard_map(shards, mesh=mesh, in_specs=in_specs, out_specs=out_specs, check_vma=False)
+    body = functools.partial(choose, mesh)
+    return jax.shard_map(body, mesh=mesh, in_specs=in_specs, out_specs=out_specs, check_vma=False)

time: 216 us -> 30.5 us (0.14)
  waiting for transfers between devices: 93.8 us -> 0 us
  blocking collectives: 83.7 us -> 0 us
  Pallas kernels: 0 us -> 25.7 us
  between operations: 14.3 us -> 0.7 us
  starting transfers between devices: 7.64 us -> 0 us
  other arithmetic: 7.02 us -> 0 us
  matrix products: 3.58 us -> 0 us
    psum x1 -> x0, waiting for transfers between devices: 86.8 us -> none  [shards(): lax.psum((dw_in_part, dgain_in_part, dbias_in_part), ('blk', 'ch', 'sub'))]
    all_gather x3 -> x0, blocking collectives: 40.7 us -> none  [the longest x1 14.6 us: shards(): lax.all_gather(left_loc, 'blk', axis=1, tiled=True)]
    psum x1 -> x0, blocking collectives: 30.6 us -> none  [shards(): lax.psum((dw_in_part, dgain_in_part, dbias_in_part), ('blk', 'ch', 'sub'))]
    pallas_call x0 -> x2, Pallas kernels: none -> 25.7 us  [the longest x1 18.9 us: fused(): pl.pallas_call(functools.partial(front_kernel, sizes, rows, width), out_s...]
    all_to_all x2 -> x0, blocking collectives: 12.4 us -> none  [the longest x1 6.2 us: shards(): lax.all_to_all(jnp.transpose(d_prod, (2, 0, 1)), ('ch', 'sub'), split_axi...]
    all_to_all x2 -> x0, starting transfers between devices: 7.6 us -> none  [the longest x1 4.21 us: shards(): lax.all_to_all(stacked, ('ch', 'sub'), split_axis=1, concat_axis=2, tiled...]
    all_to_all x2 -> x0, waiting for transfers between devices: 6.9 us -> none  [the longest x1 3.95 us: shards(): lax.all_to_all(stacked, ('ch', 'sub'), split_axis=1, concat_axis=2, tiled...]
    mul x6 -> x0, other arithmetic: 4.44 us -> none  [the longest x1 1.75 us: shards(): sums[0] * scale]
  transfers between devices with their start and end apart: 3 -> 0, of which waited for: 3 -> 0; matrix products, arithmetic and copies ran while one was open for 1% -> 0% of each run, Pallas kernels for 0% -> 0%
where the time goes in v2:
time: 30.5 us; the launch traced here: 30.2 us
  Pallas kernels  25.7 us (84%)
  local copies, waits for them, and re-layouts  3.81 us (12%)
  between operations  0.7 us (2%)
    pallas_call x1, Pallas kernels, fused(): pl.pallas_call(functools.partial(front_kernel, sizes, rows, width), out_s...  18.9 us
    pallas_call x1, Pallas kernels, fused(): pl.pallas_call(functools.partial(back_kernel, sizes, rows, width), out_sh...  6.78 us
    unnamed x20, local copies, waits for them, and re-layouts  3.81 us

profile of v2, /device:TPU:0, one launch (start us, length us, event | category | flops | bytes accessed | tf_op | source)
XLA Modules:
  0.0 30.2 jit_solution(3893527544868087996)
XLA Ops:
  0.6 0.0 copy-start.7
  0.6 0.0 copy-start.8
  0.7 0.0 copy-start.9
  0.7 0.0 copy-start.5
  0.7 0.0 copy-start.6
  0.7 0.6 %copy-done.7 = f32[128]{0:T(128)S(1)} copy-done((f32[128]{0:T(128)S(1)}, f32[128]{0:T(128)}, u32[]{:S(2)}) %copy-start.7) | copy-done | bytes 536
  1.3 0.0 copy-done.8
  1.3 0.0 copy-done.9
  1.3 0.0 copy-done.5
  1.3 0.0 copy-done.6
  1.4 0.0 copy-start
  1.4 0.9 %copy-done = bf16[128,640]{1,0:T(8,128)(2,1)S(1)} copy-done((bf16[128,640]{1,0:T(8,128)(2,1)S(1)}, bf16[128,640]{1,0:T(8,128)(2,1)}, u32[]{:S(2)}) %copy-start) | copy-done | bytes 163864
  2.3 0.0 copy-start.2
  2.3 0.7 %copy-done.2 = bf16[2,32,128]{2,1,0:T(8,128)(2,1)S(1)} copy-done((bf16[2,32,128]{2,1,0:T(8,128)(2,1)S(1)}, bf16[2,32,128]{2,1,0:T(8,128)(2,1)}, u32[]{:S(2)}) %copy-start.2) | copy-done | bytes 16408
  3.0 0.0 copy-start.3
  3.0 0.8 %copy-done.3 = bf16[128,128]{1,0:T(8,128)(2,1)S(1)} copy-done((bf16[128,128]{1,0:T(8,128)(2,1)S(1)}, bf16[128,128]{1,0:T(8,128)(2,1)}, u32[]{:S(2)}) %copy-start.3) | copy-done | bytes 32792
  3.8 0.0 copy-start.4
  3.8 0.7 %copy-done.4 = bf16[2,32,128]{2,1,0:T(8,128)(2,1)S(1)} copy-done((bf16[2,32,128]{2,1,0:T(8,128)(2,1)S(1)}, bf16[2,32,128]{2,1,0:T(8,128)(2,1)}, u32[]{:S(2)}) %copy-start.4) | copy-done | bytes 16408
  4.5 0.0 copy-start.1
  4.5 18.9 %shard_map.144 = (bf16[1024,128]{1,0:T(8,128)(2,1)S(1)}, f32[1024,128]{1,0:T(8,128)S(1)}, f32[1024,128]{1,0:T(8,128)S(1)}, f32[1024,128]{1,0:T(8,128)S(1)}, f32[...) custom-call(bf16[64,128]{1,0:T(8,128)(2,1)S(1)} %bitcast.11, ...), custom_call_target="tpu_custom_call" | custom-call | tf_op jit(solution)/shard_map/pallas_call | solution.py:439
  23.4 0.0 copy-done.1
  23.4 6.8 %shard_map.145 = (bf16[64,128]{1,0:T(8,128)(2,1)}, f32[128,640]{1,0:T(8,128)}, f32[128,128]{1,0:T(8,128)}, f32[1,128]{1,0:T(1,128)}, f32[1,128]{1,0:T(1,128)}, /*index=5*/f32[1,128]{1,0:T(1,128)}, f32[1,128]{1,0:T(1,128)}) custom-call(bf16[1024,128]{1,0:T(8,128)(2,1)S(1)} %get-tuple-element.27.xs, f32[1024,128]{1,0:T(8,128)S(1)} %get-tuple-element.28.nrm, ...), custom_call_target="tpu_custom_call" | custom-call | tf_op jit(solution)/shard_map/pallas_call | solution.py:465
Async XLA Ops:
  0.6 0.7 %copy-start.7 = (f32[128]{0:T(128)S(1)}, f32[128]{0:T(128)}, u32[]{:S(2)}) copy-start(f32[128]{0:T(128)} %param.15) | copy-start | bytes 1540
  0.6 0.7 %copy-start.8 = (f32[128]{0:T(128)S(1)}, f32[128]{0:T(128)}, u32[]{:S(2)}) copy-start(f32[128]{0:T(128)} %param.16) | copy-start | bytes 1540
  0.7 0.7 %copy-start.9 = (f32[128]{0:T(128)S(1)}, f32[128]{0:T(128)}, u32[]{:S(2)}) copy-start(f32[128]{0:T(128)} %param.17) | copy-start | bytes 1540
  0.7 0.7 %copy-start.5 = (f32[128]{0:T(128)S(1)}, f32[128]{0:T(128)}, u32[]{:S(2)}) copy-start(f32[128]{0:T(128)} %param.14) | copy-start | bytes 1540
  0.7 0.7 %copy-start.6 = (s32[2,32]{1,0:T(2,128)S(1)}, s32[2,32]{1,0:T(2,128)}, u32[]{:S(2)}) copy-start(s32[2,32]{1,0:T(2,128)} %mask_hbm.1) | copy-start | bytes 772
  1.4 0.9 %copy-start = (bf16[128,640]{1,0:T(8,128)(2,1)S(1)}, bf16[128,640]{1,0:T(8,128)(2,1)}, u32[]{:S(2)}) copy-start(bf16[128,640]{1,0:T(8,128)(2,1)} %w_in_hbm.3) | copy-start | bytes 491524
  2.3 0.7 %copy-start.2 = (bf16[2,32,128]{2,1,0:T(8,128)(2,1)S(1)}, bf16[2,32,128]{2,1,0:T(8,128)(2,1)}, u32[]{:S(2)}) copy-start(bf16[2,32,128]{2,1,0:T(8,128)(2,1)} %param.9) | copy-start | bytes 49156
  3.0 0.8 %copy-start.3 = (bf16[128,128]{1,0:T(8,128)(2,1)S(1)}, bf16[128,128]{1,0:T(8,128)(2,1)}, u32[]{:S(2)}) copy-start(bf16[128,128]{1,0:T(8,128)(2,1)} %w_out_hbm.1) | copy-start | bytes 98308
  3.8 0.7 %copy-start.4 = (bf16[2,32,128]{2,1,0:T(8,128)(2,1)S(1)}, bf16[2,32,128]{2,1,0:T(8,128)(2,1)}, u32[]{:S(2)}) copy-start(bf16[2,32,128]{2,1,0:T(8,128)(2,1)} %param.10) | copy-start | bytes 49156
  4.5 18.9 %copy-start.1 = (bf16[128,640]{1,0:T(8,128)(2,1)S(1)}, bf16[128,640]{1,0:T(8,128)(2,1)}, u32[]{:S(2)}) copy-start(bf16[128,640]{1,0:T(8,128)(2,1)} %w_in_hbm.3) | copy-start | bytes 491524

commit v3 on v2

--- a/solution.py
+++ b/solution.py
@@ -115,7 +115,7 @@
 
 MESH = pl.DeviceIdType.MESH
 PAD = 16
-VMEM_BYTES = 32 * 1024 * 1024
+VMEM_BYTES = 58 * 1024 * 1024
 
 
 def flat_slot(sizes, blk, ch, sub):
@@ -162,9 +162,9 @@
 
 def front_kernel(
     sizes, rows, width,
-    act_hbm, grad_hbm, mask_hbm, w_in_hbm, w_out_hbm, gain_in_ref, bias_in_ref, gain_mid_ref, bias_mid_ref,
+    act_hbm, grad_hbm, mask_hbm, w_in_hbm, w_out_hbm, vec_hbm,
     xs, nrm, fa, fb, ca, cb, qa, qb, dp, dpg, dw_out_ref, dgain_mid_ref, dbias_mid_ref,
-    ga, gg, mask_ref, w_in_ref, w_out_ref, sg, ys, dos, in_sem, send_sem, recv_sem, core_send,
+    ga, gg, mask_ref, w_in_ref, w_out_ref, vec_refs, sg, ys, dos, in_sem, send_sem, recv_sem, core_send,
 ):
     nz, nx, nc = sizes
     chips = nz * nx
@@ -190,6 +190,9 @@
         pltpu.make_async_copy(grad_hbm, gg.at[me], in_sem.at[2]),
         pltpu.make_async_copy(w_in_hbm, w_in_ref, in_sem.at[3]),
         pltpu.make_async_copy(w_out_hbm, w_out_ref, in_sem.at[4]),
+    ] + [
+        pltpu.make_async_copy(src, dst, in_sem.at[5 + n])
+        for n, (src, dst) in enumerate(zip(vec_hbm, vec_refs))
     ]
     for load in loads:
         load.start()
@@ -235,8 +238,9 @@
         chip_copy(which, slot, 0, peers[0]).wait_recv()
 
     send_own(0)
-    gain_in, bias_in = gain_in_ref[...], bias_in_ref[...]
-    gain_mid, bias_mid = gain_mid_ref[...], bias_mid_ref[...]
+    for load in loads[5:]:
+        load.wait()
+    gain_in, bias_in, gain_mid, bias_mid = [ref[...] for ref in vec_refs]
     at_row = lax.broadcasted_iota(jnp.int32, (width, chan), 0)
     at_lane = lax.broadcasted_iota(jnp.int32, (width, chan), 1)
     on_diag = at_row == at_lane
@@ -354,27 +358,14 @@
             core_copy(which, me, n).wait_send()
 
 
-def back_kernel(
-    sizes, rows, width,
-    xs, nrm, fa, fb, ca, cb, qa, qb, dp, dpg, dwo, dgm, dbm, act_hbm, w_in_hbm, gain_in_ref,
-    d_pair_ref, dw_in_ref, dw_out_ref, dgain_in_ref, dbias_in_ref, dgain_mid_ref, dbias_mid_ref,
-    dpr, dxs, act_ref, w_in_ref, in_sem,
+def back_part(
+    sizes, rows, width, xs, nrm, fa, fb, ca, cb, qa, qb, dp, dpg, ga, w_in_ref, gain_in_ref,
+    d_pair_ref, dw_in_ref, dgain_in_ref, dbias_in_ref, dpr, dxs,
 ):
     pairs = rows * width
     hid, chan = fa.shape[1], nrm.shape[1]
     scale = 1.0 / width
-    loads = [
-        pltpu.make_async_copy(w_in_hbm, w_in_ref, in_sem.at[0]),
-        pltpu.make_async_copy(act_hbm, act_ref, in_sem.at[1]),
-    ]
-    for load in loads:
-        load.start()
     me = flat_slot(sizes, lax.axis_index("blk"), lax.axis_index("ch"), lax.axis_index("sub"))
-    dw_out_ref[...] = dwo[...]
-    dgain_mid_ref[...] = dgm[...]
-    dbias_mid_ref[...] = dbm[...]
-    for load in loads:
-        load.wait()
     block = 8
     big = block * width
 
@@ -412,13 +403,53 @@
     dgain_in_ref[...] = dgain * scale
     dbias_in_ref[...] = dbias * scale
     dw_in_ref[...] = t_dot(xs[...], dpr[...]) * scale
-    _, inverse = norm_rows(act_ref[...].astype(jnp.float32))
+    _, inverse = norm_rows(ga[me, :pairs, :].astype(jnp.float32))
     own = pl.ds(pl.multiple_of(me * pairs, pairs), pairs)
     normed = nrm[own, :]
     v = dxs[own, :] * gain_in_ref[...]
     d_pair_ref[...] = (inverse * (v - lane_mean(v) - normed * lane_mean(v * normed))).astype(
         jnp.bfloat16
     )
+
+
+def whole_kernel(
+    sizes, rows, width,
+    act_hbm, grad_hbm, mask_hbm, w_in_hbm, w_out_hbm, gain_in_hbm, bias_in_hbm, gain_mid_hbm, bias_mid_hbm,
+    d_pair_ref, dw_in_ref, dw_out_ref, dgain_in_ref, dbias_in_ref, dgain_mid_ref, dbias_mid_ref,
+    xs, nrm, fa, fb, ca, cb, qa, qb, dp, dpg, dpr, dxs,
+    ga, gg, mask_ref, w_in_ref, w_out_ref, gain_in_ref, bias_in_ref, gain_mid_ref, bias_mid_ref,
+    sg, ys, dos, in_sem, send_sem, recv_sem, core_send,
+):
+    front_kernel(
+        sizes, rows, width, act_hbm, grad_hbm, mask_hbm, w_in_hbm, w_out_hbm,
+        (gain_in_hbm, bias_in_hbm, gain_mid_hbm, bias_mid_hbm),
+        xs, nrm, fa, fb, ca, cb, qa, qb, dp, dpg, dw_out_ref, dgain_mid_ref, dbias_mid_ref,
+        ga, gg, mask_ref, w_in_ref, w_out_ref,
+        (gain_in_ref, bias_in_ref, gain_mid_ref, bias_mid_ref),
+        sg, ys, dos, in_sem, send_sem, recv_sem, core_send,
+    )
+    back_part(
+        sizes, rows, width, xs, nrm, fa, fb, ca, cb, qa, qb, dp, dpg, ga, w_in_ref, gain_in_ref,
+        d_pair_ref, dw_in_ref, dgain_in_ref, dbias_in_ref, dpr, dxs,
+    )
+
+
+def finish_kernel(count, *refs):
+    sems = refs[-1]
+    loads = [
+        pltpu.make_async_copy(refs[n], refs[2 * count + n], sems.at[0, n]) for n in range(count)
+    ]
+    stores = [
+        pltpu.make_async_copy(refs[2 * count + n], refs[count + n], sems.at[1, n])
+        for n in range(count)
+    ]
+    for load in loads:
+        load.start()
+    for load, store in zip(loads, stores):
+        load.wait()
+        store.start()
+    for store in stores:
+        store.wait()
 
 
 def fused(sizes, pair_act, pair_grad, pair_mask, w_in, w_out, gain_in, bias_in, gain_mid, bias_mid):
@@ -431,26 +462,34 @@
     f32, low = jnp.float32, jnp.bfloat16
     vmem = pl.BlockSpec(memory_space=pltpu.VMEM)
     hbm = pl.BlockSpec(memory_space=pltpu.HBM)
-    act = pair_act.reshape(pairs, chan)
-    gain_row = gain_in.reshape(1, chan)
     vector = jax.ShapeDtypeStruct((1, hid), f32)
-    big = jax.ShapeDtypeStruct((full, hid), f32)
-    big_low = jax.ShapeDtypeStruct((full, hid), low)
-    kept = pl.pallas_call(
-        functools.partial(front_kernel, sizes, rows, width),
-        out_shape=(big_low,) + (big,) * 8 + (big_low, jax.ShapeDtypeStruct(w_out.shape, f32), vector, vector),
-        in_specs=[hbm] * 5 + [vmem] * 4,
-        out_specs=(vmem,) * 13,
-        scratch_shapes=[
+    out = pl.pallas_call(
+        functools.partial(whole_kernel, sizes, rows, width),
+        out_shape=(
+            jax.ShapeDtypeStruct((pairs, chan), low),
+            jax.ShapeDtypeStruct(w_in.shape, f32),
+            jax.ShapeDtypeStruct(w_out.shape, f32),
+        ) + (vector,) * 4,
+        in_specs=[hbm] * 9,
+        out_specs=(vmem,) * 7,
+        scratch_shapes=[pltpu.VMEM((full, chan), low)]
+        + [pltpu.VMEM((full, hid), f32)] * 8
+        + [
+            pltpu.VMEM((full, hid), low),
+            pltpu.VMEM((full, w_in.shape[1]), low),
+            pltpu.VMEM((full, chan), f32),
             pltpu.VMEM((slots, pairs + PAD, chan), low),
             pltpu.VMEM((slots, pairs, chan), low),
             pltpu.VMEM((rows, width), jnp.int32),
             pltpu.VMEM(w_in.shape, low),
             pltpu.VMEM(w_out.shape, low),
+        ]
+        + [pltpu.VMEM((1, chan), f32)] * 4
+        + [
             pltpu.VMEM((full, chan), f32),
             pltpu.VMEM((full, hid), low),
             pltpu.VMEM((full, chan), low),
-            pltpu.SemaphoreType.DMA((5,)),
+            pltpu.SemaphoreType.DMA((9,)),
             pltpu.SemaphoreType.DMA((2, chips)),
             pltpu.SemaphoreType.DMA((2, slots)),
             pltpu.SemaphoreType.DMA((2, slots)),
@@ -459,27 +498,20 @@
             collective_id=0, has_side_effects=True, vmem_limit_bytes=VMEM_BYTES
         ),
     )(
-        act, pair_grad.reshape(pairs, chan), pair_mask, w_in, w_out, gain_row,
-        bias_in.reshape(1, chan), gain_mid.reshape(1, hid), bias_mid.reshape(1, hid),
-    )
+        pair_act.reshape(pairs, chan), pair_grad.reshape(pairs, chan), pair_mask, w_in, w_out,
+        gain_in.reshape(1, chan), bias_in.reshape(1, chan),
+        gain_mid.reshape(1, hid), bias_mid.reshape(1, hid),
+    )
+    anywhere = pl.BlockSpec(memory_space=pl.ANY)
     out = pl.pallas_call(
-        functools.partial(back_kernel, sizes, rows, width),
-        out_shape=(
-            jax.ShapeDtypeStruct((pairs, chan), low),
-            jax.ShapeDtypeStruct(w_in.shape, f32),
-            jax.ShapeDtypeStruct(w_out.shape, f32),
-        ) + (vector,) * 4,
-        in_specs=[vmem] * 13 + [hbm, hbm, vmem],
-        out_specs=(vmem,) * 7,
-        scratch_shapes=[
-            pltpu.VMEM((full, w_in.shape[1]), low),
-            pltpu.VMEM((full, chan), f32),
-            pltpu.VMEM((pairs, chan), low),
-            pltpu.VMEM(w_in.shape, low),
-            pltpu.SemaphoreType.DMA((2,)),
-        ],
+        functools.partial(finish_kernel, len(out)),
+        out_shape=tuple(jax.ShapeDtypeStruct(piece.shape, piece.dtype) for piece in out),
+        in_specs=[anywhere] * len(out),
+        out_specs=(anywhere,) * len(out),
+        scratch_shapes=[pltpu.VMEM(piece.shape, piece.dtype) for piece in out]
+        + [pltpu.SemaphoreType.DMA((2, len(out)))],
         compiler_params=pltpu.CompilerParams(vmem_limit_bytes=VMEM_BYTES),
-    )(*kept, act, w_in, gain_row)
+    )(*out)
     return (out[0].reshape(rows, width, chan), out[1], out[2]) + tuple(
         piece.reshape(-1) for piece in out[3:]
     )

time: 30.5 us -> 28.1 us (0.921)
  local copies, waits for them, and re-layouts: 3.81 us -> 0 us
  Pallas kernels: 25.7 us -> 27.2 us
    unnamed x20 -> x0, local copies, waits for them, and re-layouts: 3.81 us -> none
    pallas_call x2, Pallas kernels: 25.7 us -> 27.2 us  [the longest x1 25.3 us: fused(): pl.pallas_call(functools.partial(whole_kernel, sizes, rows, width), out_s...]
where the time goes in v3:
time: 28.1 us; the launch traced here: 27.8 us
  Pallas kernels  27.2 us (97%)
  between operations  0.64 us (2%)
    pallas_call x1, Pallas kernels, fused(): pl.pallas_call(functools.partial(whole_kernel, sizes, rows, width), out_s...  25.3 us
    pallas_call x1, Pallas kernels, fused(): pl.pallas_call(functools.partial(finish_kernel, len(out)), out_shape=tupl...  1.86 us

profile of v3, /device:TPU:0, one launch (start us, length us, event | category | flops | bytes accessed | tf_op | source)
XLA Modules:
  0.0 27.8 jit_solution(12546397292627599363)
XLA Ops:
  0.6 25.3 %shard_map.144 = (bf16[64,128]{1,0:T(8,128)(2,1)}, f32[128,640]{1,0:T(8,128)}, f32[128,128]{1,0:T(8,128)}, f32[1,128]{1,0:T(1,128)}, f32[1,128]{1,0:T(1,128)}, /*index=5*/f32[1,128]{1,0:T(1,128)}, f32[1,128]{1,0:T(1,128)}) custom-call(bf16[64,128]{1,0:T(8,128)(2,1)} %bitcast.11, bf16[64,128]{1,0:T(8,128)(2,1)} %bitcast.12, s32[2,32]{1,0:T(2,128)} %mask_hbm.1, ...), custom_call_target="tpu_custom_call" | custom-call | tf_op jit(solution)/shard_map/pallas_call | solution.py:466
  26.0 1.9 %shard_map.145 = (bf16[64,128]{1,0:T(8,128)(2,1)}, f32[128,640]{1,0:T(8,128)}, f32[128,128]{1,0:T(8,128)}, f32[1,128]{1,0:T(1,128)}, f32[1,128]{1,0:T(1,128)}, /*index=5*/f32[1,128]{1,0:T(1,128)}, f32[1,128]{1,0:T(1,128)}) custom-call(bf16[64,128]{1,0:T(8,128)(2,1)} %get-tuple-element.21.refs_0_, f32[128,640]{1,0:T(8,128)} %get-tuple-element.22.refs_1_, ...), custom_call_target="tpu_custom_call" | custom-call | tf_op jit(solution)/shard_map/pallas_call | solution.py:506

commit v4 on v3

--- a/solution.py
+++ b/solution.py
@@ -361,55 +361,90 @@
 def back_part(
     sizes, rows, width, xs, nrm, fa, fb, ca, cb, qa, qb, dp, dpg, ga, w_in_ref, gain_in_ref,
     d_pair_ref, dw_in_ref, dgain_in_ref, dbias_in_ref, dpr, dxs,
+    part_out, part_in, vec_out, vec_in, half_send, half_recv,
 ):
+    nc = sizes[2]
     pairs = rows * width
     hid, chan = fa.shape[1], nrm.shape[1]
     scale = 1.0 / width
-    me = flat_slot(sizes, lax.axis_index("blk"), lax.axis_index("ch"), lax.axis_index("sub"))
+    z, x, c = lax.axis_index("blk"), lax.axis_index("ch"), lax.axis_index("sub")
+    me = flat_slot(sizes, z, x, c)
+    other = (lax.axis_index("grp"), z, x, lax.rem(c + 1, nc))
     block = 8
     big = block * width
+    per_block = block // rows
+    blocks = width // block // nc
+
+    def slot_rows(n):
+        return pl.ds(pl.multiple_of((n * nc + c) * pairs, pairs), pairs)
 
     def back(kb, sums):
         dgain, dbias = sums
-        base = kb * block
-        here = pl.ds(pl.multiple_of(base * width, big), big)
+        here = pl.ds(pl.multiple_of(kb * big, big), big)
+
+        def pick(ref):
+            return jnp.concatenate(
+                [ref[slot_rows(kb * per_block + q), :] for q in range(per_block)], axis=0
+            )
+
+        def line(p):
+            return ((kb * per_block + p // rows) * nc + c) * pairs + (p % rows) * width
+
         left = outer_sum(
             width,
-            lambda p, j: fb[pl.ds((base + p) * width + j, 1), :],
+            lambda p, j: fb[pl.ds(line(p) + j, 1), :],
             lambda j: dp[pl.ds(j, width, stride=width), :],
             width, hid, block,
         )
         grad = jnp.concatenate(left, axis=0).astype(jnp.bfloat16).astype(jnp.float32)
-        dpr[here, :hid] = (grad * qa[here, :]).astype(jnp.bfloat16)
-        dpr[here, hid : 2 * hid] = (grad * ca[here, :]).astype(jnp.bfloat16)
+        dpr[here, :hid] = (grad * pick(qa)).astype(jnp.bfloat16)
+        dpr[here, hid : 2 * hid] = (grad * pick(ca)).astype(jnp.bfloat16)
         right = outer_sum(
             width,
-            lambda p, i: fa[pl.ds((base + p) * width + i, 1), :],
+            lambda p, i: fa[pl.ds(line(p) + i, 1), :],
             lambda i: dp[pl.ds(pl.multiple_of(i * width, width), width), :],
             width, hid, block,
         )
         grad = jnp.concatenate(right, axis=0).astype(jnp.bfloat16).astype(jnp.float32)
-        dpr[here, 2 * hid : 3 * hid] = (grad * qb[here, :]).astype(jnp.bfloat16)
-        dpr[here, 3 * hid : 4 * hid] = (grad * cb[here, :]).astype(jnp.bfloat16)
-        dpr[here, 4 * hid :] = dpg[here, :]
+        dpr[here, 2 * hid : 3 * hid] = (grad * pick(qb)).astype(jnp.bfloat16)
+        dpr[here, 3 * hid : 4 * hid] = (grad * pick(cb)).astype(jnp.bfloat16)
+        dpr[here, 4 * hid :] = pick(dpg)
         d_x = dot_t(dpr[here, :], w_in_ref[...])
         dxs[here, :] = d_x
-        dgain = dgain + jnp.sum(d_x * nrm[here, :], axis=0, keepdims=True)
+        dgain = dgain + jnp.sum(d_x * pick(nrm), axis=0, keepdims=True)
         dbias = dbias + jnp.sum(d_x, axis=0, keepdims=True)
         return dgain, dbias
 
     none = jnp.zeros((1, chan), jnp.float32)
-    dgain, dbias = lax.fori_loop(0, width // block, back, (none, none))
-    dgain_in_ref[...] = dgain * scale
-    dbias_in_ref[...] = dbias * scale
-    dw_in_ref[...] = t_dot(xs[...], dpr[...]) * scale
+    dgain, dbias = lax.fori_loop(0, blocks, back, (none, none))
+    vec_out[0:8, :] = jnp.broadcast_to(dgain, (8, chan))
+    vec_out[8:16, :] = jnp.broadcast_to(dbias, (8, chan))
+    x_half = jnp.concatenate([xs[slot_rows(n), :] for n in range(sizes[0] * sizes[1])], axis=0)
+    part_out[...] = t_dot(x_half, dpr[...]).astype(jnp.bfloat16)
+    swaps = [
+        pltpu.make_async_remote_copy(
+            src_ref=src, dst_ref=dst, send_sem=half_send.at[n], recv_sem=half_recv.at[n],
+            device_id=other, device_id_type=MESH,
+        )
+        for n, (src, dst) in enumerate(((part_out, part_in), (vec_out, vec_in)))
+    ]
+    for swap in swaps:
+        swap.start()
     _, inverse = norm_rows(ga[me, :pairs, :].astype(jnp.float32))
     own = pl.ds(pl.multiple_of(me * pairs, pairs), pairs)
+    kept = pl.ds(pl.multiple_of(me // nc * pairs, pairs), pairs)
     normed = nrm[own, :]
-    v = dxs[own, :] * gain_in_ref[...]
+    v = dxs[kept, :] * gain_in_ref[...]
     d_pair_ref[...] = (inverse * (v - lane_mean(v) - normed * lane_mean(v * normed))).astype(
         jnp.bfloat16
     )
+    for swap in swaps:
+        swap.wait()
+    dw_in_ref[...] = (
+        part_out[...].astype(jnp.float32) + part_in[...].astype(jnp.float32)
+    ) * scale
+    dgain_in_ref[...] = (vec_out[0:1, :] + vec_in[0:1, :]) * scale
+    dbias_in_ref[...] = (vec_out[8:9, :] + vec_in[8:9, :]) * scale
 
 
 def whole_kernel(
@@ -419,6 +454,7 @@
     xs, nrm, fa, fb, ca, cb, qa, qb, dp, dpg, dpr, dxs,
     ga, gg, mask_ref, w_in_ref, w_out_ref, gain_in_ref, bias_in_ref, gain_mid_ref, bias_mid_ref,
     sg, ys, dos, in_sem, send_sem, recv_sem, core_send,
+    part_out, part_in, vec_out, vec_in, half_send, half_recv,
 ):
     front_kernel(
         sizes, rows, width, act_hbm, grad_hbm, mask_hbm, w_in_hbm, w_out_hbm,
@@ -431,6 +467,7 @@
     back_part(
         sizes, rows, width, xs, nrm, fa, fb, ca, cb, qa, qb, dp, dpg, ga, w_in_ref, gain_in_ref,
         d_pair_ref, dw_in_ref, dgain_in_ref, dbias_in_ref, dpr, dxs,
+        part_out, part_in, vec_out, vec_in, half_send, half_recv,
     )
 
 
@@ -476,8 +513,8 @@
         + [pltpu.VMEM((full, hid), f32)] * 8
         + [
             pltpu.VMEM((full, hid), low),
-            pltpu.VMEM((full, w_in.shape[1]), low),
-            pltpu.VMEM((full, chan), f32),
+            pltpu.VMEM((full // sizes[2], w_in.shape[1]), low),
+            pltpu.VMEM((full // sizes[2], chan), f32),
             pltpu.VMEM((slots, pairs + PAD, chan), low),
             pltpu.VMEM((slots, pairs, chan), low),
             pltpu.VMEM((rows, width), jnp.int32),
@@ -493,6 +530,12 @@
             pltpu.SemaphoreType.DMA((2, chips)),
             pltpu.SemaphoreType.DMA((2, slots)),
             pltpu.SemaphoreType.DMA((2, slots)),
+            pltpu.VMEM(w_in.shape, low),
+            pltpu.VMEM(w_in.shape, low),
+            pltpu.VMEM((16, chan), f32),
+            pltpu.VMEM((16, chan), f32),
+            pltpu.SemaphoreType.DMA((2,)),
+            pltpu.SemaphoreType.DMA((2,)),
         ],
         compiler_params=pltpu.CompilerParams(
             collective_id=0, has_side_effects=True, vmem_limit_bytes=VMEM_BYTES
@@ -521,7 +564,7 @@
     rows, width, chan = args[0].shape
     sizes = (mesh.shape["blk"], mesh.shape["ch"], mesh.shape["sub"])
     fits = width * width * chan * 128 <= VMEM_BYTES
-    whole = width % 32 == 0 and 8 % rows == 0 and chan >= width and chan == 128 and args[4].shape[0] == 128
+    whole = sizes[2] == 2 and width % 32 == 0 and 8 % rows == 0 and chan >= width and chan == 128 and args[4].shape[0] == 128
     if fits and whole and rows * sizes[0] * sizes[1] * sizes[2] == width:
         return fused(sizes, *args)
     return shards(*args)

time: 28.1 us -> 26.5 us (0.943)
  Pallas kernels: 27.2 us -> 25.5 us
    pallas_call x1, Pallas kernels: 25.3 us -> 23.7 us  [fused(): pl.pallas_call(functools.partial(whole_kernel, sizes, rows, width), out_s...]
where the time goes in v4:
time: 26.5 us; the launch traced here: 26.2 us
  Pallas kernels  25.5 us (96%)
  between operations  0.64 us (2%)
    pallas_call x1, Pallas kernels, fused(): pl.pallas_call(functools.partial(whole_kernel, sizes, rows, width), out_s...  23.7 us
    pallas_call x1, Pallas kernels, fused(): pl.pallas_call(functools.partial(finish_kernel, len(out)), out_shape=tupl...  1.86 us

profile of v4, /device:TPU:0, one launch (start us, length us, event | category | flops | bytes accessed | tf_op | source)
XLA Modules:
  0.0 26.2 jit_solution(6646095178358433147)
XLA Ops:
  0.6 23.7 %shard_map.144 = (bf16[64,128]{1,0:T(8,128)(2,1)}, f32[128,640]{1,0:T(8,128)}, f32[128,128]{1,0:T(8,128)}, f32[1,128]{1,0:T(1,128)}, f32[1,128]{1,0:T(1,128)}, /*index=5*/f32[1,128]{1,0:T(1,128)}, f32[1,128]{1,0:T(1,128)}) custom-call(bf16[64,128]{1,0:T(8,128)(2,1)} %bitcast.11, bf16[64,128]{1,0:T(8,128)(2,1)} %bitcast.12, s32[2,32]{1,0:T(2,128)} %mask_hbm.1, ...), custom_call_target="tpu_custom_call" | custom-call | tf_op jit(solution)/shard_map/pallas_call | solution.py:503
  24.3 1.9 %shard_map.145 = (bf16[64,128]{1,0:T(8,128)(2,1)}, f32[128,640]{1,0:T(8,128)}, f32[128,128]{1,0:T(8,128)}, f32[1,128]{1,0:T(1,128)}, f32[1,128]{1,0:T(1,128)}, /*index=5*/f32[1,128]{1,0:T(1,128)}, f32[1,128]{1,0:T(1,128)}) custom-call(bf16[64,128]{1,0:T(8,128)(2,1)} %get-tuple-element.21.refs_0_, f32[128,640]{1,0:T(8,128)} %get-tuple-element.22.refs_1_, ...), custom_call_target="tpu_custom_call" | custom-call | tf_op jit(solution)/shard_map/pallas_call | solution.py:549

commit v5 on v4

--- a/solution.py
+++ b/solution.py
@@ -145,7 +145,7 @@
 
 
 def outer_sum(length, row_of, vec_of, width, chan, block):
-    step = 4
+    step = 8
 
     def body(t, acc):
         acc = list(acc)
@@ -238,6 +238,8 @@
         chip_copy(which, slot, 0, peers[0]).wait_recv()
 
     send_own(0)
+    loads[2].wait()
+    send_own(1)
     for load in loads[5:]:
         load.wait()
     gain_in, bias_in, gain_mid, bias_mid = [ref[...] for ref in vec_refs]
@@ -280,10 +282,8 @@
         put(sg, sigm(proj[:, 4 * hid :]))
 
     loads[3].wait()
-    loads[2].wait()
     for n in range(1, nz):
         take(0, n)
-    send_own(1)
     for r in range(nx):
         if r:
             for n in range(r * nz, (r + 1) * nz):

time: 26.5 us -> 25.2 us (0.951)
  Pallas kernels: 25.5 us -> 24.2 us
    pallas_call x1, Pallas kernels: 23.7 us -> 22.4 us  [fused(): pl.pallas_call(functools.partial(whole_kernel, sizes, rows, width), out_s...]
where the time goes in v5:
time: 25.2 us; the launch traced here: 24.9 us
  Pallas kernels  24.2 us (96%)
  between operations  0.64 us (3%)
    pallas_call x1, Pallas kernels, fused(): pl.pallas_call(functools.partial(whole_kernel, sizes, rows, width), out_s...  22.4 us
    pallas_call x1, Pallas kernels, fused(): pl.pallas_call(functools.partial(finish_kernel, len(out)), out_shape=tupl...  1.86 us

profile of v5, /device:TPU:0, one launch (start us, length us, event | category | flops | bytes accessed | tf_op | source)
XLA Modules:
  0.0 24.9 jit_solution(1093363921294345707)
XLA Ops:
  0.6 22.4 %shard_map.144 = (bf16[64,128]{1,0:T(8,128)(2,1)}, f32[128,640]{1,0:T(8,128)}, f32[128,128]{1,0:T(8,128)}, f32[1,128]{1,0:T(1,128)}, f32[1,128]{1,0:T(1,128)}, /*index=5*/f32[1,128]{1,0:T(1,128)}, f32[1,128]{1,0:T(1,128)}) custom-call(bf16[64,128]{1,0:T(8,128)(2,1)} %bitcast.11, bf16[64,128]{1,0:T(8,128)(2,1)} %bitcast.12, s32[2,32]{1,0:T(2,128)} %mask_hbm.1, ...), custom_call_target="tpu_custom_call" | custom-call | tf_op jit(solution)/shard_map/pallas_call | solution.py:503
  23.0 1.9 %shard_map.145 = (bf16[64,128]{1,0:T(8,128)(2,1)}, f32[128,640]{1,0:T(8,128)}, f32[128,128]{1,0:T(8,128)}, f32[1,128]{1,0:T(1,128)}, f32[1,128]{1,0:T(1,128)}, /*index=5*/f32[1,128]{1,0:T(1,128)}, f32[1,128]{1,0:T(1,128)}) custom-call(bf16[64,128]{1,0:T(8,128)(2,1)} %get-tuple-element.21.refs_0_, f32[128,640]{1,0:T(8,128)} %get-tuple-element.22.refs_1_, ...), custom_call_target="tpu_custom_call" | custom-call | tf_op jit(solution)/shard_map/pallas_call | solution.py:549
